TPU v7x, 512 devices: a whole 4x8x8 slice. The times are simulated.
512 devices in a mesh: dp: 64 (over x, z, core), tensor: 8 (over y).
Axes of the slice: x: 4, y: 8, z: 8, core: 2. Of those that a mesh axis runs over, the one named last changes fastest.
Arguments:
- queries: bfloat16 [32768, 2048], P('dp', 'tensor'), may hold values from -18 to 18, as said below
- key_rows: bfloat16 [32768, 2048], P('dp', 'tensor'), may hold values from -18 to 18
- value_rows: bfloat16 [32768, 2048], P('dp', 'tensor'), may hold values from -6 to 6
- out_grad: bfloat16 [32768, 2048], P('dp', 'tensor'), may hold values from -6 to 6
- qkv_weight: bfloat16 [3, 4096, 2048], P(None, 'dp', 'tensor'), may hold values from -0.078125 to 0.078125
- row_owner: int32 [32768, 3], P('dp'), may hold values from 0 to 63, all different within a row; in each aligned block of 512 rows (0 to 511, 512 to 1023, ...) at most 48 rows name the same one
- row_hash: int32 [32768, 3], P('dp'), may hold values from 0 to 1048575
- live_rows: int32 [64], replicated, may hold values from 128 to 512, as said below
Outputs:
- table_grad: bfloat16 [32768, 4096], P('dp', 'tensor')
Inputs may be any that keep to these rules, and one draw needn't show every extreme that they name: The hidden law may align a few queries with keys at their own and the previous position. `row_owner`: the three rows of a token go to three different owners; among the rows of one device, no owner is named by more than 48 tokens, a bound that some block reaches. `live_rows`: multiples of 128; some owner has exactly 512.
All inputs are finite; a program needn't handle non-finite values.
Results may differ from a plain program's by a relative error of at most 0.02.
Values may be sent and summed in bfloat16 or wider, within the bound.
A program may use at most 64 MiB of HBM per device.

v0:
```python
import jax
import jax.numpy as jnp
from jax import lax
from jax.sharding import PartitionSpec as P

HD = 128
SLOTS = 512


def attention_backward(queries, key_rows, value_rows, out_grad):
    length = queries.shape[0]
    head_count = queries.shape[1] // HD
    query_heads = queries.reshape(length, head_count, HD)
    key_heads = key_rows.reshape(length, head_count, HD)
    value_heads = value_rows.reshape(length, head_count, HD)
    grad_heads = out_grad.reshape(length, head_count, HD)
    factor = HD ** (-0.5)
    scores = (
        jnp.einsum("qhc,khc->hqk", query_heads, key_heads, preferred_element_type=jnp.float32)
        * factor
    )
    causal = jnp.arange(length)[:, None] >= jnp.arange(length)[None, :]
    scores = jnp.where(causal[None], scores, -jnp.inf)
    highest = jnp.max(scores, axis=-1, keepdims=True)
    weights = jnp.exp(scores - highest)
    probs = weights / jnp.sum(weights, axis=-1, keepdims=True)
    probs_half = probs.astype(jnp.bfloat16)
    grad_value = jnp.einsum(
        "hqk,qhc->khc", probs_half, grad_heads, preferred_element_type=jnp.float32
    )
    grad_probs = jnp.einsum(
        "qhc,khc->hqk", grad_heads, value_heads, preferred_element_type=jnp.float32
    )
    delta = jnp.sum(probs * grad_probs, axis=-1, keepdims=True)
    grad_scores = (probs * (grad_probs - delta) * factor).astype(jnp.bfloat16)
    grad_query = jnp.einsum(
        "hqk,khc->qhc", grad_scores, key_heads, preferred_element_type=jnp.float32
    )
    grad_key = jnp.einsum(
        "hqk,qhc->khc", grad_scores, query_heads, preferred_element_type=jnp.float32
    )
    stacked = jnp.stack(
        [
            grad_query.astype(jnp.bfloat16),
            grad_key.astype(jnp.bfloat16),
            grad_value.astype(jnp.bfloat16),
        ]
    )
    return stacked.reshape(3, length, head_count * HD)


def local(queries, key_rows, value_rows, out_grad, qkv_weight, row_owner, row_hash, live_rows):
    grads = attention_backward(queries, key_rows, value_rows, out_grad)
    whole_weight = lax.all_gather(qkv_weight, "dp", axis=1, tiled=True)
    partial_value = jnp.einsum(
        "jtc,jrc->tr", grads, whole_weight, preferred_element_type=jnp.float32
    )
    input_grad = lax.psum_scatter(
        partial_value.astype(jnp.bfloat16), "tensor", scatter_dimension=1, tiled=True
    )
    owner_count = lax.axis_size("dp")
    tokens_here, columns = input_grad.shape
    capacity = 6 * tokens_here // owner_count
    flat_owner = row_owner.reshape(-1)
    picks = flat_owner[:, None] == jnp.arange(owner_count, dtype=jnp.int32)[None, :]
    live_of = jnp.sum(jnp.where(picks, live_rows[None, :], 0), axis=1)
    running = jnp.cumsum(picks.astype(jnp.int32), axis=0) - 1
    within = jnp.sum(jnp.where(picks, running, 0), axis=1)
    target = flat_owner * capacity + within
    slot_index = row_hash.reshape(-1) % live_of
    sources = jnp.repeat(input_grad, 3, axis=0)
    outgoing = jnp.zeros((owner_count * capacity, columns), jnp.bfloat16).at[target].set(sources)
    slot_out = jnp.full((owner_count * capacity,), SLOTS, jnp.int32).at[target].set(slot_index)
    arrived, arrived_slots = (
        lax.all_to_all(
            outgoing.reshape(owner_count, capacity, columns),
            "dp",
            split_axis=0,
            concat_axis=0,
            tiled=True,
        ),
        lax.all_to_all(
            slot_out.reshape(owner_count, capacity), "dp", split_axis=0, concat_axis=0, tiled=True
        ),
    )
    table = (
        jnp.zeros((SLOTS, columns), jnp.float32)
        .at[arrived_slots.reshape(-1)]
        .add(arrived.reshape(-1, columns).astype(jnp.float32), mode="drop")
    )
    return table.astype(jnp.bfloat16)


def solution(mesh):
    return jax.shard_map(
        local,
        mesh=mesh,
        in_specs=(
            P("dp", "tensor"),
            P("dp", "tensor"),
            P("dp", "tensor"),
            P("dp", "tensor"),
            P(None, "dp", "tensor"),
            P("dp", None),
            P("dp", None),
            P(),
        ),
        out_specs=P("dp", "tensor"),
        check_vma=False,
    )
```

profile of v0, /device:TPU:1, one launch (start us, length us, event | category | flops | bytes accessed | tf_op | source)
XLA Modules:
  0.0 292.8 jit_solution(9037026670181445218)
XLA Ops:
  6.5 0.7 all-gather.2.cloned.1.call-update
  7.3 0.0 reduce-scatter.2.cloned.1.call-start
  7.3 1.1 copy.64
  8.4 1.1 copy.65
  9.5 1.1 copy.66
  10.6 0.1 iota_compare_fusion
  10.7 0.0 copy-start.1
  10.7 0.4 fusion.37
  11.1 2.3 fusion.52
  13.4 3.9 %fusion.16 = bf16[2,512,128]{1,2,0:T(8,128)(2,1)} fusion(bf16[512,2,128]{0,2,1:T(8,128)(2,1)S(1)} %bitcast.55, f32[2,512,512]{1,2,0:T(8,128)S(1)} %fusion.37, f32[2,512,512]{1,2,0:T(8,128)} %get-tuple-element.8, f32[2,512]{1,0:T(2,128)S(1)} %get-tuple-element.7), kind=kOutput, calls=%fused_computation.18 | convolution fusion | flops 138020352 | bytes 4722688 | tf_op jit(solution)/shard_map/hqk,khc->qhc/dot_general | solution.py:36
  17.4 1.1 copy.58
  18.5 3.8 %fusion.19 = bf16[2,512,128]{1,2,0:T(8,128)(2,1)} fusion(bf16[512,2,128]{0,2,1:T(8,128)(2,1)S(1)} %bitcast.58, f32[2,512,512]{1,2,0:T(8,128)S(1)} %fusion.37, f32[2,512,512]{1,2,0:T(8,128)} %get-tuple-element.8, f32[2,512]{1,0:T(2,128)S(1)} %get-tuple-element.7), kind=kOutput, calls=%fused_computation.19 | convolution fusion | flops 138020352 | bytes 4722688 | tf_op jit(solution)/shard_map/hqk,qhc->khc/dot_general | solution.py:39
  22.3 1.1 copy.59
  23.4 2.3 convolution_convert_fusion
  25.6 0.1 copy.60
  25.8 78.0 %all-gather.2.cloned.1.call-done = bf16[3,4096,256]{2,1,0:T(8,128)(2,1)} async-done(((bf16[3,64,256]{2,1,0:T(8,128)(2,1)}), bf16[3,4096,256]{2,1,0:T(8,128)(2,1)}) %all-gather.2.cloned.1.call-update) | async-done | bytes 6291472 | tf_op jit(solution)/shard_map/all_gather | solution.py:54
  103.8 7.8 %bitcast_convert_fusion = bf16[512,4096]{1,0:T(8,128)(2,1)} fusion(bf16[3,4096,256]{2,1,0:T(8,128)(2,1)} %all-gather.2.cloned.1.call-done, bf16[1,512,256]{2,1,0:T(8,128)(2,1)S(1)} %copy.60, bf16[1,512,256]{2,1,0:T(8,128)(2,1)S(1)} %copy.59, bf16[1,512,256]{2,1,0:T(8,128)(2,1)S(1)} %copy.58), kind=kOutput, calls=%fused_computation.5 | convolution fusion | flops 3224109056 | bytes 11272192 | tf_op jit(solution)/shard_map/jtc,jrc->tr/dot_general | solution.py:55
  111.6 0.0 reduce-scatter.2.cloned.1.call-update
  111.6 0.7 copy-done.2
  112.3 0.1 copy.42
  112.5 0.0 copy-start.3
  112.5 0.2 eq.33
  112.7 0.2 eq.29
  112.9 18.1 %reduce-window.6 = s32[64,12,128]{2,1,0:T(8,128)S(1)} reduce-window(s32[64,12,128]{2,1,0:T(8,128)S(1)} %fusion.34, s32[]{:T(128)} %constant.5.clone.1), window={size=1x1x128 pad=0_0x0_0x127_0}, to_apply=%region_0.1 | reduce-window | flops 12484608 | bytes 786436 | tf_op jit(solution)/shard_map/reduce-window
  131.1 0.2 slice.8
  131.3 0.3 copy.44
  131.6 0.1 copy.45
  131.7 0.1 copy.41
  131.8 0.2 mul.30
  132.1 0.1 copy.46
  132.2 0.2 reshape.132
  132.5 0.2 add_add_fusion
  132.7 0.2 select_reduce_fusion
  132.9 0.1 add_select_fusion
  133.0 6.2 %scatter_custom_fusion = s32[3072]{0:T(1024)S(1)} fusion(s32[1536]{0:T(1024)S(1)} %fusion.42, s32[1536]{0:T(1024)S(1)} %add_select_fusion, s32[]{:T(128)} %constant.11.clone.1), kind=kCustom, calls=%fused_computation.52 | custom fusion | bytes 12292 | tf_op jit(solution)/shard_map/scatter | solution.py:73
  139.2 0.7 all_to_all.9
  139.9 5.6 %all-to-all-start = ((s32[64,1,48]{2,1,0:T(1,128)}), s32[64,1,48]{2,1,0:T(1,128)S(1)}, u32[]{:S(2)}, u32[]{:S(2)}) async-start(s32[64,1,48]{2,1,0:T(1,128)} %bitcast.2), calls=%async_computation | async-start | bytes 65536 | tf_op jit(solution)/shard_map/all_to_all | solution.py:82
  145.5 19.8 %reduce-scatter.2.cloned.1.call-done = bf16[512,512]{1,0:T(8,128)(2,1)} async-done(((bf16[512,4096]{1,0:T(8,128)(2,1)}), bf16[512,512]{1,0:T(8,128)(2,1)}) %reduce-scatter.2.cloned.1.call-update) | async-done | bytes 524304 | tf_op jit(solution)/shard_map/reduce_scatter | solution.py:58
  165.3 1.6 broadcast_in_dim.57
  166.9 2.5 reshape.153
  169.4 9.9 %scatter_custom_fusion.1 = bf16[3072,512]{1,0:T(8,128)(2,1)} fusion(s32[1536]{0:T(1024)S(1)} %fusion.42, bf16[1536,512]{1,0:T(8,128)(2,1)} %reshape.153, bf16[]{:T(256)} %constant.7.clone.1), kind=kCustom, calls=%fused_computation.16 | custom fusion | bytes 3146240 | tf_op jit(solution)/shard_map/scatter | solution.py:72
  179.3 11.1 %all-to-all-start.1 = ((bf16[64,48,512]{2,1,0:T(8,128)(2,1)}), bf16[64,48,512]{2,1,0:T(8,128)(2,1)S(1)}, u32[]{:S(2)}, u32[]{:S(2)}) async-start(bf16[64,48,512]{2,1,0:T(8,128)(2,1)} %bitcast.11), calls=%async_computation.2 | async-start | bytes 6291456 | tf_op jit(solution)/shard_map/all_to_all | solution.py:75
  190.4 0.5 broadcast.119
  190.9 0.7 reduce.5
  191.6 0.1 reshape.133
  191.8 72.1 %all-to-all-done.1 = bf16[64,48,512]{2,1,0:T(8,128)(2,1)S(1)} async-done(((bf16[64,48,512]{2,1,0:T(8,128)(2,1)}), bf16[64,48,512]{2,1,0:T(8,128)(2,1)S(1)}, u32[]{:S(2)}, u32[]{:S(2)}) %all-to-all-start.1) | async-done | bytes 3145760 | tf_op jit(solution)/shard_map/all_to_all | solution.py:75
  263.9 19.9 %scatter_custom_fusion.2 = f32[512,512]{1,0:T(8,128)} fusion(s32[3072]{0:T(1024)S(1)} %bitcast.65, bf16[3072,512]{1,0:T(8,128)(2,1)S(1)} %bitcast.50, f32[]{:T(128)} %constant.10.clone.1), kind=kCustom, calls=%fused_computation.6 | custom fusion | flops 3145728 | bytes 4194308 | tf_op jit(solution)/shard_map/scatter-add | solution.py:89
  283.8 2.1 convert_element_type.53
  (14 shorter events, 0.1 us)
Async XLA Ops:
  6.5 4.2 %copy-start = (bf16[512,256]{1,0:T(8,128)(2,1)S(1)}, bf16[512,256]{1,0:T(8,128)(2,1)}, u32[]{:S(2)}) copy-start(bf16[512,256]{1,0:T(8,128)(2,1)} %param.10) | copy-start | bytes 786436
  6.5 97.2 %all-gather.2.cloned.1.call-start = ((), (), s32[]{:S(2)}) async-start(), calls=%async_computation.3 | async-start | bytes 6389760 | tf_op jit(solution)/shard_map/all_gather | solution.py:54
  7.3 158.1 %reduce-scatter.2.cloned.1.call-start = ((), (), s32[]{:S(2)}) async-start(), calls=%async_computation.4 | async-start | bytes 4718592 | tf_op jit(solution)/shard_map/reduce_scatter | solution.py:58
  10.7 2.7 copy-start.1
  111.6 0.7 copy-start.2
  112.5 19.6 %copy-start.3 = (s32[512,3]{0,1:T(4,128)S(1)}, s32[512,3]{0,1:T(4,128)}, u32[]{:S(2)}) copy-start(s32[512,3]{0,1:T(4,128)} %param.14) | copy-start | bytes 18436
  131.1 1.6 copy-start.4
  139.9 39.4 %all-to-all-start = ((s32[64,1,48]{2,1,0:T(1,128)}), s32[64,1,48]{2,1,0:T(1,128)S(1)}, u32[]{:S(2)}, u32[]{:S(2)}) async-start(s32[64,1,48]{2,1,0:T(1,128)} %bitcast.2), calls=%async_computation | async-start | bytes 65536 | tf_op jit(solution)/shard_map/all_to_all | solution.py:82
  179.3 84.6 %all-to-all-start.1 = ((bf16[64,48,512]{2,1,0:T(8,128)(2,1)}), bf16[64,48,512]{2,1,0:T(8,128)(2,1)S(1)}, u32[]{:S(2)}, u32[]{:S(2)}) async-start(bf16[64,48,512]{2,1,0:T(8,128)(2,1)} %bitcast.11), calls=%async_computation.2 | async-start | bytes 6291456 | tf_op jit(solution)/shard_map/all_to_all | solution.py:75
Sparse Core Ops, SparseCore 0:
  10.7 92.9 all-gather.1
  111.8 53.5 reduce-scatter.1
where the time goes:
time: 293 us
  waiting for transfers between devices  171 us (58%)
  other arithmetic  41.6 us (14%)
  local copies, waits for them, and re-layouts  29.6 us (10%)
  matrix products  20.6 us (7%)
  starting transfers between devices  16.7 us (6%)
  between operations  13.6 us (5%)
    all_gather x1, waiting for transfers between devices, local(): whole_weight = lax.all_gather(qkv_weight, 'dp', axis=1, tiled=True)  78 us
    all_to_all x1, waiting for transfers between devices, local(): lax.all_to_all(outgoing.reshape(owner_count, capacity, columns), 'dp', sp...  72.1 us
    scatter-add x1, other arithmetic, local(): table = jnp.zeros((SLOTS, columns), jnp.float32).at[arrived_slots.reshape...  19.9 us
    reduce_scatter x1, waiting for transfers between devices, local(): lax.psum_scatter(partial_value.astype(jnp.bfloat16), 'tensor', scatter_di...  19.8 us
    another operation x2, other arithmetic  18.2 us
    all_to_all x1, starting transfers between devices, local(): lax.all_to_all(outgoing.reshape(owner_count, capacity, columns), 'dp', sp...  11.1 us
    scatter x1, local copies, waits for them, and re-layouts, local(): jnp.zeros((owner_count * capacity, columns), jnp.bfloat16).at[target]  9.9 us
    dot_general x1, matrix products, local(): jnp.einsum('jtc,jrc->tr', grads, whole_weight, preferred_element_type=jnp...  7.85 us
  transfers between devices with their start and end apart: 4, of which 3 were waited for; matrix products, arithmetic and copies ran while one was open for 21% of the time, Pallas kernels for 0%

commit v1 on v0

v1 whole, which is shorter than its diff:
```python
import functools

import jax
import jax.numpy as jnp
from jax import lax
from jax.experimental import pallas as pl
from jax.experimental.pallas import tpu as pltpu
from jax.sharding import PartitionSpec as P

MESH = pl.DeviceIdType.MESH
F32, BF16, I32 = jnp.float32, jnp.bfloat16, jnp.int32
HD = 128
LANES = 128
QB = 128
NX, NZ, NY, CORES = 4, 8, 8, 2
SLOTS = 512
CAP = 48
STRIDE = 2


def nt(a, b):
    return lax.dot_general(a, b, (((1,), (1,)), ((), ())), preferred_element_type=F32)


def nn(a, b):
    return lax.dot_general(a, b, (((1,), (0,)), ((), ())), preferred_element_type=F32)


def tn(a, b):
    return lax.dot_general(a, b, (((0,), (0,)), ((), ())), preferred_element_type=F32)


def iota(shape, axis):
    return lax.broadcasted_iota(I32, shape, axis)


def attention(q_ref, k_ref, v_ref, do_ref, grads, dk_acc, dv_acc):
    tokens, width = q_ref.shape
    factor = HD ** (-0.5)
    for head in range(width // HD):
        cols = slice(head * HD, (head + 1) * HD)
        for block in range(tokens // QB):
            rows = slice(block * QB, (block + 1) * QB)
            reach = (block + 1) * QB
            q, do = q_ref[rows, cols], do_ref[rows, cols]
            k, v = k_ref[:reach, cols], v_ref[:reach, cols]
            scores = nt(q, k) * factor
            seen = iota((QB, reach), 0) + block * QB >= iota((QB, reach), 1)
            scores = jnp.where(seen, scores, -jnp.inf)
            weights = jnp.exp(scores - jnp.max(scores, axis=1, keepdims=True))
            probs = weights * (1.0 / jnp.sum(weights, axis=1, keepdims=True))
            grad_probs = nt(do, v)
            delta = jnp.sum(probs * grad_probs, axis=1, keepdims=True)
            grad_scores = (probs * (grad_probs - delta) * factor).astype(BF16)
            grads[0, rows, cols] = nn(grad_scores, k).astype(BF16)
            dk, dv = tn(grad_scores, q), tn(probs.astype(BF16), do)
            if block > 0:
                dk_acc[: reach - QB] += dk[: reach - QB]
                dv_acc[: reach - QB] += dv[: reach - QB]
            dk_acc[reach - QB : reach] = dk[reach - QB :]
            dv_acc[reach - QB : reach] = dv[reach - QB :]
        grads[1, :, cols] = dk_acc[...].astype(BF16)
        grads[2, :, cols] = dv_acc[...].astype(BF16)


def kernel(
    q_ref, k_ref, v_ref, do_ref, w_ref, meta_ref, live_ref, out_ref,
    grads, dk_acc, dv_acc, wbuf, tbuf, mbuf, ysend, yrecv, zsend, zrecv,
    upper, p1, p2, cslot, cbuf, tfin,
    wz_s, wz_r, m_s, m_r, wx_s, wx_r, wc_s, wc_r, tx_s, tx_r, tc_s, tc_r, ys_s, ys_r, zs_s, zs_r,
):
    tokens = q_ref.shape[0]
    nc, wr = wbuf.shape[0], wbuf.shape[4]
    per_block = NX * NZ // NY
    mx, my, mz = NX // 2, NY // 2, NZ // 2
    sources = CORES * NX
    dp, y = lax.axis_index("dp"), lax.axis_index("tensor")
    c, chip = lax.rem(dp, CORES), dp // CORES
    z, x = lax.rem(chip, NZ), chip // NZ

    def at(x_, z_, c_):
        return ((lax.rem(x_ + NX, NX) * NZ + lax.rem(z_ + NZ, NZ)) * CORES + lax.rem(c_, CORES), y)

    def row(y_):
        return (dp, lax.rem(y_ + NY, NY))

    def copy(src, dst, ssem, rsem, where):
        return pltpu.make_async_remote_copy(
            src_ref=src, dst_ref=dst, send_sem=ssem, recv_sem=rsem, device_id=where, device_id_type=MESH
        )

    sibling = at(x, z, c + 1)
    x_right, x_left = at(x + 1, z, c), at(x - 1, z, c)
    plane = [(dx, dc) for dx in range(NX) for dc in range(CORES) if (dx, dc) != (0, 0)]
    z_order = sorted(range(1, NZ), key=lambda k: -min(k, NZ - k))

    barrier = pltpu.get_barrier_semaphore()
    peers = [at(x + dx, z, c + dc) for dx, dc in plane]
    peers += [at(x, z + k, c) for k in range(1, NZ)]
    peers += [row(y + 1), row(y - 1)]
    for peer in peers:
        pl.semaphore_signal(barrier, inc=1, device_id=peer, device_id_type=MESH)
    pl.semaphore_wait(barrier, len(peers))

    def wz_copy(j, k):
        return copy(
            w_ref.at[:, pl.ds(pl.multiple_of(j * wr, wr), wr), :], wbuf.at[j, :, c, chip],
            wz_s.at[j, k - 1], wz_r.at[j, k - 1], at(x, z + k, c),
        )

    for j in range(nc):
        for k in z_order:
            wz_copy(j, k).start()

    owner, hashed = meta_ref[0:3, :], meta_ref[3:6, :]
    live = jnp.zeros_like(owner)
    for o in range(NX * NZ * CORES):
        live = jnp.where(owner == o, live_ref[o], live)
    high, blocks = hashed >> 7, live >> 7
    third = high - 3 * ((high * 21846) >> 16)
    high = jnp.where(blocks == 3, third, high & (blocks - 1))
    mbuf[c, x, 0:3, :] = owner
    mbuf[c, x, 3:6, :] = (hashed & 127) + high * 128
    mbuf[c, x, 6:8, :] = jnp.zeros((2, tokens), I32)

    def meta_copy(i):
        dx, dc = plane[i]
        return copy(mbuf.at[c, x], mbuf.at[c, x], m_s.at[i], m_r.at[i], at(x + dx, z, c + dc))

    for i in range(len(plane)):
        meta_copy(i).start()

    for j in range(nc):
        wbuf[j, :, c, chip] = w_ref[:, j * wr : (j + 1) * wr, :]

    attention(q_ref, k_ref, v_ref, do_ref, grads, dk_acc, dv_acc)

    upper[...] = jnp.where(iota((tokens, tokens), 0) < iota((tokens, tokens), 1), 1.0, 0.0).astype(BF16)
    for i in range(len(plane)):
        meta_copy(i).wait_recv()
    mine = (x * NZ + iota((NZ, tokens), 0)) * CORES + c
    entries = NZ * CAP

    def pick_body(source, carry):
        part = mbuf.at[source // NX, lax.rem(source, NX)]
        hits = [part[n : n + 1, :] == mine for n in range(3)]
        slot = jnp.zeros((NZ, tokens), I32)
        named = jnp.zeros((NZ, tokens), F32)
        for n in range(3):
            slot = jnp.where(hits[n], part[n + 3 : n + 4, :], slot)
            named = jnp.where(hits[n], 1.0, named)
        rank = nn(named.astype(BF16), upper[...])
        code = jnp.where(named > 0.5, rank, -1.0).astype(I32)
        for b in range(NZ):
            p1[source, b * CAP : (b + 1) * CAP, :] = jnp.where(
                code[b : b + 1, :] == iota((CAP, tokens), 0), 1.0, 0.0
            ).astype(BF16)
        halves = jnp.concatenate([slot & 255, slot >> 8], axis=0).astype(F32).astype(BF16)
        moved = nt(halves, p1[source])
        own = iota((NZ, entries), 0) * CAP
        at_entry = iota((NZ, entries), 1)
        inside = (at_entry >= own) & (at_entry < own + CAP)
        cslot[0, pl.ds(source, 1), :] = jnp.sum(jnp.where(inside, moved[:NZ], 0.0), axis=0, keepdims=True)
        cslot[1, pl.ds(source, 1), :] = jnp.sum(jnp.where(inside, moved[NZ:], 0.0), axis=0, keepdims=True)
        return carry

    lax.fori_loop(0, sources, pick_body, 0)
    deep = sources * CAP

    def slot_body(b, carry):
        entry = iota((sources, deep), 1)
        first = iota((sources, deep), 0) * CAP
        inside = (entry >= first) & (entry < first + CAP)
        rank = entry[:1] - jnp.sum(jnp.where(entry >= first, CAP, 0), axis=0, keepdims=True) + CAP
        spread = jnp.where(iota((entries, deep), 0) == rank + b * CAP, 1.0, 0.0).astype(BF16)
        low = nn(cslot[0].astype(BF16), spread)
        top = nn(cslot[1].astype(BF16), spread)
        slot = jnp.sum(jnp.where(inside, low + 256.0 * top, 0.0), axis=0, keepdims=True).astype(I32)
        p2[b] = jnp.where(iota((SLOTS, deep), 0) == slot, 1.0, 0.0).astype(BF16)
        return carry

    lax.fori_loop(0, NZ, slot_body, 0)

    class Gather:
        def __init__(self, piece, sems):
            self.piece, (self.xs, self.xr, self.cs, self.cr) = piece, sems

        def hop(self, j, k, side):
            origin = lax.rem(x + NX - (k - 1) if side == 0 else x + k - 1, NX)
            part = None if k < mx else side
            ref = self.piece(j, c, origin, part)
            i = 2 * (k - 1) + side
            return copy(ref, ref, self.xs.at[j, i], self.xr.at[j, i], x_right if side == 0 else x_left)

        def arrival(self, j, k, side):
            origin = lax.rem(x + NX - k if side == 0 else x + k, NX)
            part = None if k < mx else side
            ref = self.piece(j, c, origin, part)
            i = 2 * (k - 1) + side
            return copy(ref, ref, self.xs.at[j, i], self.xr.at[j, i], x_right if side == 0 else x_left)

        def across(self, j, d):
            ref = self.piece(j, c, lax.rem(x + d, NX), None)
            return copy(ref, ref, self.cs.at[j, d], self.cr.at[j, d], sibling)

        def crossed(self, j, d):
            ref = self.piece(j, lax.rem(c + 1, CORES), lax.rem(x + d, NX), None)
            return copy(ref, ref, self.cs.at[j, d], self.cr.at[j, d], sibling)

        def stage(self, j, k):
            if k > 0:
                for side in range(2):
                    self.arrival(j, k, side).wait_recv()
            if k < mx:
                for side in range(2):
                    self.hop(j, k + 1, side).start()
            if k == 0 or k == mx:
                self.across(j, k).start()
            else:
                self.across(j, k).start()
                self.across(j, NX - k).start()

        def finish(self, j):
            for d in range(NX):
                self.crossed(j, d).wait_recv()

        def drain(self, j):
            for k in range(1, mx + 1):
                for side in range(2):
                    self.hop(j, k, side).wait_send()
            for d in range(NX):
                self.across(j, d).wait_send()

    def w_piece(j, c_, x_, part):
        start, count = (0, NZ) if part is None else (part * (NZ // 2), NZ // 2)
        return wbuf.at[j, :, c_, pl.ds(x_ * NZ + start, count)]

    def t_piece(j, c_, x_, part):
        start, count = (0, tokens) if part is None else (part * (tokens // 2), tokens // 2)
        return tbuf.at[j, c_, x_, pl.ds(start, count)]

    weights = Gather(w_piece, (wx_s, wx_r, wc_s, wc_r))
    gathered = Gather(t_piece, (tx_s, tx_r, tc_s, tc_r))

    class Ring:
        def __init__(self, me, n, left, right, partial, done, bufs, sems):
            self.me, self.n, self.m = me, n, n // 2
            self.left, self.right, self.partial, self.done = left, right, partial, done
            (self.out, self.inc), (self.ss, self.rs) = bufs, sems
            self.rows = self.out.shape[3]

        def hop(self, j, s, side):
            half = self.rows // 2
            part = pl.ds(side * half, half) if s == 0 else pl.ds(0, self.rows)
            return copy(
                self.out.at[side, j, s, part], self.inc.at[side, j, s, part],
                self.ss.at[side, j, s], self.rs.at[side, j, s], self.left if side == 0 else self.right,
            )

        def step(self, j, s):
            half, m, n = self.rows // 2, self.m, self.n
            parts = (slice(0, half), slice(half, self.rows))
            if s == 0:
                value = self.partial(j, lax.rem(self.me + m, n)).astype(BF16)
                for side in range(2):
                    self.out[side, j, 0, parts[side], :] = value[parts[side]]
                    self.hop(j, 0, side).start()
            elif s < m:
                for side in range(2):
                    block = lax.rem(self.me + n + (s - m if side == 0 else m - s), n)
                    value = self.partial(j, block)
                    self.hop(j, s - 1, side).wait_recv()
                    if s == 1:
                        near, far = parts[side], parts[1 - side]
                        self.out[side, j, s, near, :] = (value[near] + self.inc[side, j, 0, near, :].astype(F32)).astype(BF16)
                        self.out[side, j, s, far, :] = value[far].astype(BF16)
                    else:
                        self.out[side, j, s] = (value + self.inc[side, j, s - 1].astype(F32)).astype(BF16)
                    self.hop(j, s, side).start()
            else:
                value = self.partial(j, self.me)
                for side in range(2):
                    self.hop(j, m - 1, side).wait_recv()
                if m == 1:
                    value = value + jnp.concatenate([self.inc[i, j, 0, parts[i], :].astype(F32) for i in range(2)], axis=0)
                else:
                    value = value + self.inc[0, j, m - 1].astype(F32) + self.inc[1, j, m - 1].astype(F32)
                self.done(j, value.astype(BF16))

        def drain(self, j):
            for s in range(self.m):
                for side in range(2):
                    self.hop(j, s, side).wait_send()

    def y_partial(j, block):
        total = None
        for i in range(3):
            w = [wbuf[j, i, c_, pl.ds(block * per_block, per_block)].reshape(per_block * wr, -1) for c_ in range(CORES)]
            term = nt(grads[i], jnp.concatenate(w, axis=0))
            total = term if total is None else total + term
        return total

    def y_done(j, value):
        tbuf[j, c, x] = value

    def z_partial(j, block):
        return nn(p2[block], cbuf[j, block])

    def z_done(j, value):
        tfin[j] = value

    def compact(j):
        def body(source, carry):
            picked = nn(p1[source], tbuf[j, source // NX, lax.rem(source, NX)]).astype(BF16)
            start = pl.multiple_of(source * CAP, CAP)
            for b in range(NZ):
                cbuf[j, b, pl.ds(start, CAP), :] = picked[b * CAP : (b + 1) * CAP]
            return carry

        lax.fori_loop(0, sources, body, 0)

    ring_y = Ring(y, NY, row(y - 1), row(y + 1), y_partial, y_done, (ysend, yrecv), (ys_s, ys_r))
    ring_z = Ring(z, NZ, at(x, z - 1, c), at(x, z + 1, c), z_partial, z_done, (zsend, zrecv), (zs_s, zs_r))

    def w_stage(k):
        def run(j):
            if k == 0:
                for far in range(1, NZ):
                    copy(wbuf.at[j, :, c, chip], wbuf.at[j, :, c, x * NZ + lax.rem(z + NZ - far, NZ)],
                         wz_s.at[j, far - 1], wz_r.at[j, far - 1], sibling).wait_recv()
            weights.stage(j, k)
        return run

    y_base = mx + 1
    z_base = y_base + my + mx + 1
    plan = []
    for s in range(my - 1, 0, -1):
        plan.append((y_base + s, functools.partial(lambda s, j: ring_y.step(j, s), s)))
    plan.append((y_base + my, lambda j: (ring_y.step(j, my), gathered.stage(j, 0))))
    for k in range(1, mx + 1):
        plan.append((y_base + my + k, functools.partial(lambda k, j: gathered.stage(j, k), k)))
    for s in range(mz, 0, -1):
        plan.append((z_base + s, functools.partial(lambda s, j: ring_z.step(j, s), s)))
    plan.append((z_base, lambda j: (gathered.finish(j), compact(j), ring_z.step(j, 0))))
    plan.append((y_base, lambda j: (weights.finish(j), ring_y.step(j, 0))))
    for k in range(mx, -1, -1):
        plan.append((k, w_stage(k)))

    def iteration(t, carry):
        for start, run in plan:
            ahead = t - start
            j = ahead // STRIDE

            @pl.when((ahead >= 0) & (ahead < nc * STRIDE) & (ahead - j * STRIDE == 0))
            def _():
                run(j)

        return carry

    lax.fori_loop(0, z_base + mz + (nc - 1) * STRIDE + 1, iteration, 0)

    width = out_ref.shape[1]
    shard = wr * nc
    p = iota((LANES, width), 0)
    group = per_block * wr
    home = shard * (CORES * (lax.rem(p, group) // wr) + p // group) + lax.rem(p, wr)
    total = None
    for j in range(nc):
        order = jnp.where(home + wr * j == iota((LANES, width), 1), 1.0, 0.0).astype(BF16)
        term = nn(tfin[j], order)
        total = term if total is None else total + term
    out_ref[...] = total.astype(BF16)

    for i in range(len(plane)):
        meta_copy(i).wait_send()

    def drain(j, carry):
        for k in range(1, NZ):
            wz_copy(j, k).wait_send()
        weights.drain(j)
        gathered.drain(j)
        ring_y.drain(j)
        ring_z.drain(j)
        return carry

    lax.fori_loop(0, nc, drain, 0)


def local(queries, key_rows, value_rows, out_grad, qkv_weight, row_owner, row_hash, live_rows):
    tokens, features = queries.shape
    shard = qkv_weight.shape[1]
    per_block = NX * NZ // NY
    wr = LANES // (CORES * per_block)
    nc = shard // wr
    my, mz, mx = NY // 2, NZ // 2, NX // 2
    meta = jnp.concatenate([row_owner.T, row_hash.T, jnp.zeros((2, tokens), I32)], axis=0)
    dma = lambda *shape: pltpu.SemaphoreType.DMA(shape)
    vmem = pl.BlockSpec(memory_space=pltpu.VMEM)
    sources = CORES * NX
    return pl.pallas_call(
        kernel,
        out_shape=jax.ShapeDtypeStruct((SLOTS, nc * LANES), BF16),
        in_specs=[vmem] * 6 + [pl.BlockSpec(memory_space=pltpu.SMEM)],
        out_specs=vmem,
        scratch_shapes=[
            pltpu.VMEM((3, tokens, features), BF16),
            pltpu.VMEM((tokens, HD), F32),
            pltpu.VMEM((tokens, HD), F32),
            pltpu.VMEM((nc, 3, CORES, NX * NZ, wr, features), BF16),
            pltpu.VMEM((nc, CORES, NX, tokens, LANES), BF16),
            pltpu.VMEM((CORES, NX, 8, tokens), I32),
            pltpu.VMEM((2, nc, my, tokens, LANES), BF16),
            pltpu.VMEM((2, nc, my, tokens, LANES), BF16),
            pltpu.VMEM((2, nc, mz, SLOTS, LANES), BF16),
            pltpu.VMEM((2, nc, mz, SLOTS, LANES), BF16),
            pltpu.VMEM((tokens, tokens), BF16),
            pltpu.VMEM((sources, NZ * CAP, tokens), BF16),
            pltpu.VMEM((NZ, SLOTS, sources * CAP), BF16),
            pltpu.VMEM((2, sources, NZ * CAP), F32),
            pltpu.VMEM((nc, NZ, sources * CAP, LANES), BF16),
            pltpu.VMEM((nc, SLOTS, LANES), BF16),
            dma(nc, NZ - 1), dma(nc, NZ - 1),
            dma(sources - 1), dma(sources - 1),
            dma(nc, 2 * mx), dma(nc, 2 * mx), dma(nc, NX), dma(nc, NX),
            dma(nc, 2 * mx), dma(nc, 2 * mx), dma(nc, NX), dma(nc, NX),
            dma(2, nc, my), dma(2, nc, my), dma(2, nc, mz), dma(2, nc, mz),
        ],
        compiler_params=pltpu.CompilerParams(
            collective_id=0, has_side_effects=True, vmem_limit_bytes=60 * 1024 * 1024
        ),
    )(queries, key_rows, value_rows, out_grad, qkv_weight, meta, live_rows)


def solution(mesh):
    return jax.shard_map(
        local,
        mesh=mesh,
        in_specs=(
            P("dp", "tensor"),
            P("dp", "tensor"),
            P("dp", "tensor"),
            P("dp", "tensor"),
            P(None, "dp", "tensor"),
            P("dp", None),
            P("dp", None),
            P(),
        ),
        out_specs=P("dp", "tensor"),
        check_vma=False,
    )
```

time: 293 us -> 151 us (0.52)
  the two profiles are of different devices: /device:TPU:1 before, /device:TPU:6 now
where the time goes in v1:
time: 151 us
  Pallas kernels  147 us (97%)
  local copies, waits for them, and re-layouts  1.95 us (1%)
    pallas_call x1, Pallas kernels, local(): pl.pallas_call(kernel, out_shape=jax.ShapeDtypeStruct((SLOTS, nc * LANES)...  147 us

profile of v1, /device:TPU:6, one launch (start us, length us, event | category | flops | bytes accessed | tf_op | source)
XLA Modules:
  0.0 150.6 jit_solution(7188535286765374031)
XLA Ops:
  0.0 0.1 pad.2.clone
  0.1 1.4 add_add_fusion.meta_ref
  1.5 147.3 %shard_map.82 = bf16[512,512]{1,0:T(8,128)(2,1)} custom-call(bf16[512,256]{1,0:T(8,128)(2,1)} %q_ref.1, bf16[512,256]{1,0:T(8,128)(2,1)} %k_ref.1, bf16[512,256]{1,0:T(8,128)(2,1)} %v_ref.1, bf16[512,256]{1,0:T(8,128)(2,1)} %do_ref.1, bf16[3,64,256]{2,1,0:T(8,128)(2,1)} %w_ref.1, s32[8,512]{1,0:T(8,128)} %add_add_fusion.meta_ref, s32[64]{0:T(128)} %live_ref.1), custom_call_target="tpu_custom_call" | custom-call | tf_op jit(solution)/shard_map/pallas_call | solution.py:400
  148.7 1.9 %copy.10 = bf16[512,512]{1,0:T(8,128)(2,1)} copy(bf16[512,512]{1,0:T(8,128)(2,1)} %shard_map.82) | data formatting | bytes 1048576
  (1 shorter events, 0.0 us)

commit v2 on v0

v2 whole, which is shorter than its diff:
```python
import functools

import jax
import jax.numpy as jnp
from jax import lax
from jax.experimental import pallas as pl
from jax.experimental.pallas import tpu as pltpu
from jax.sharding import PartitionSpec as P

MESH = pl.DeviceIdType.MESH
F32, BF16, I32 = jnp.float32, jnp.bfloat16, jnp.int32
HD = 128
LANES = 128
QB = 128
NX, NZ, NY, CORES = 4, 8, 8, 2
SLOTS = 512
CAP = 48
PIECES = 2
NAMES = ("Y0", "Y1", "Y2", "Y3", "Y4", "XB", "C", "Z0", "Z1", "Z2", "Z3", "Z4", "WA", "WX", "WB", "WC", "att", "picks", "slots")
ORDER = (
    52, 64, 48, 65, 53, 68, 60, 56, 49, 54, 0, 72, 4, 61, 50, 57, 55, 1, 8, 5,
    62, 51, 58, 12, 2, 9, 16, 6, 63, 59, 13, 3, 10, 20, 17, 7, 24, 28, 14, 11,
    21, 32, 25, 18, 29, 15, 36, 33, 19, 22, 37, 40, 26, 23, 30, 41, 27, 31, 34, 44,
    35, 38, 45, 39, 42, 43, 46, 47,
)


def nt(a, b):
    return lax.dot_general(a, b, (((1,), (1,)), ((), ())), preferred_element_type=F32)


def nn(a, b):
    return lax.dot_general(a, b, (((1,), (0,)), ((), ())), preferred_element_type=F32)


def tn(a, b):
    return lax.dot_general(a, b, (((0,), (0,)), ((), ())), preferred_element_type=F32)


def iota(shape, axis):
    return lax.broadcasted_iota(I32, shape, axis)


def attention(head, q_ref, k_ref, v_ref, do_ref, grads, dk_acc, dv_acc):
    tokens = q_ref.shape[0]
    factor = HD ** (-0.5)
    cols = slice(head * HD, (head + 1) * HD)
    for block in range(tokens // QB):
        rows = slice(block * QB, (block + 1) * QB)
        reach = (block + 1) * QB
        q, do = q_ref[rows, cols], do_ref[rows, cols]
        k, v = k_ref[:reach, cols], v_ref[:reach, cols]
        scores = nt(q, k) * factor
        seen = iota((QB, reach), 0) + block * QB >= iota((QB, reach), 1)
        scores = jnp.where(seen, scores, -jnp.inf)
        weights = jnp.exp(scores - jnp.max(scores, axis=1, keepdims=True))
        probs = weights * (1.0 / jnp.sum(weights, axis=1, keepdims=True))
        grad_probs = nt(do, v)
        delta = jnp.sum(probs * grad_probs, axis=1, keepdims=True)
        grad_scores = (probs * (grad_probs - delta) * factor).astype(BF16)
        grads[0, rows, cols] = nn(grad_scores, k).astype(BF16)
        dk, dv = tn(grad_scores, q), tn(probs.astype(BF16), do)
        if block > 0:
            dk_acc[: reach - QB] += dk[: reach - QB]
            dv_acc[: reach - QB] += dv[: reach - QB]
        dk_acc[reach - QB : reach] = dk[reach - QB :]
        dv_acc[reach - QB : reach] = dv[reach - QB :]
    grads[1, :, cols] = dk_acc[...].astype(BF16)
    grads[2, :, cols] = dv_acc[...].astype(BF16)


class Ring:
    def __init__(self, copy, me, n, left, right, partial, done, out, inc, ss, rs):
        self.copy, self.me, self.n, self.m = copy, me, n, n // 2
        self.to, self.partial, self.done = (left, right), partial, done
        self.out, self.inc, self.ss, self.rs = out, inc, ss, rs
        self.size = out.shape[3] // PIECES

    def rows(self, h, side=None):
        if side is None:
            return h * self.size, self.size
        return h * self.size + side * (self.size // 2), self.size // 2

    def hop(self, j, s, h, side):
        part = pl.ds(*self.rows(h, side if s == 0 else None))
        return self.copy(
            self.out.at[j, s, side, part], self.inc.at[j, s, side, part], self.ss.at[j, h], self.rs.at[j, h, s], self.to[side]
        )

    def both(self, j, s, h):
        part = pl.ds(*self.rows(h))
        ref = self.inc.at[j, 0, 0, part] if s == 0 else self.inc.at[j, s, :, part]
        return self.copy(ref, ref, self.ss.at[j, h], self.rs.at[j, h, s], self.to[0])

    def step(self, s, j):
        m, n, out, inc = self.m, self.n, self.out, self.inc
        if s == 0:
            value = self.partial(j, lax.rem(self.me + m, n)).astype(BF16)
            for h in range(PIECES):
                for side in range(2):
                    start, count = self.rows(h, side)
                    out[j, 0, side, start : start + count, :] = value[start : start + count]
                    self.hop(j, 0, h, side).start()
            return
        if s < m:
            values = [
                self.partial(j, lax.rem(self.me + n + (s - m if side == 0 else m - s), n)).astype(BF16)
                for side in range(2)
            ]
        else:
            values = [self.partial(j, self.me)]
        for h in range(PIECES):
            self.both(j, s - 1, h).wait_recv()
            self.both(j, s - 1, h).wait_send()
            start, count = self.rows(h)
            whole = slice(start, start + count)
            halves = [slice(first, first + size) for first, size in (self.rows(h, 0), self.rows(h, 1))]
            if s == m:
                value = values[0][whole]
                if m == 1:
                    value = value + jnp.concatenate([inc[j, 0, side, halves[side], :].astype(F32) for side in range(2)], axis=0)
                else:
                    value = value + inc[j, m - 1, 0, whole, :].astype(F32) + inc[j, m - 1, 1, whole, :].astype(F32)
                self.done(j, h, value.astype(BF16))
                continue
            for side, value in enumerate(values):
                if s == 1:
                    near, far = halves[side], halves[1 - side]
                    out[j, s, side, near, :] = value[near] + inc[j, 0, side, near, :]
                    out[j, s, side, far, :] = value[far]
                else:
                    out[j, s, side, whole, :] = value[whole] + inc[j, s - 1, side, whole, :]
                self.hop(j, s, h, side).start()


def kernel(
    q_hbm, k_hbm, v_hbm, do_hbm, w_hbm, owner_ref, hash_ref, live_ref, out_ref,
    q_ref, k_ref, v_ref, do_ref, grads, dk_acc, dv_acc, wbuf, tbuf, mbuf, ysend, yrecv, zsend, zrecv,
    upper, p1, p2, cslot, cbuf, tfin, order,
    in_s, own_s, wz_s, wz_r, wx_s, wx_r, wzx_s, wzx_r, wxz_s, wxz_r, wc_s, wc_r,
    m_s, m_r, tx_s, tx_r, tc_s, tc_r, ys_s, ys_r, zs_s, zs_r,
):
    tokens = q_ref.shape[0]
    nc, wr = wbuf.shape[0], wbuf.shape[5]
    per_block = NX * NZ // NY
    my, mz = NY // 2, NZ // 2
    sources = CORES * NX
    trows = tokens // PIECES
    dp, y = lax.axis_index("dp"), lax.axis_index("tensor")
    c, chip = lax.rem(dp, CORES), dp // CORES
    z, x = lax.rem(chip, NZ), chip // NZ

    def at(x_, z_, c_):
        return ((lax.rem(x_ + NX, NX) * NZ + lax.rem(z_ + NZ, NZ)) * CORES + lax.rem(c_, CORES), y)

    def row(y_):
        return (dp, lax.rem(y_ + NY, NY))

    def copy(src, dst, ssem, rsem, where):
        return pltpu.make_async_remote_copy(
            src_ref=src, dst_ref=dst, send_sem=ssem, recv_sem=rsem, device_id=where, device_id_type=MESH
        )

    sibling = at(x, z, c + 1)
    plane = [(dx, dc) for dx in range(NX) for dc in range(CORES) if (dx, dc) != (0, 0)]
    z_far = sorted(range(1, NZ), key=lambda k: -min(k, NZ - k))
    x_far = sorted(range(1, NX), key=lambda k: -min(k, NX - k))

    barrier = pltpu.get_barrier_semaphore()
    peers = [at(x, z + k, c) for k in z_far]
    peers += [at(x + dx, z, c + dc) for dx, dc in plane]
    peers += [row(y + 1), row(y - 1)]
    for peer in peers:
        pl.semaphore_signal(barrier, inc=1, device_id=peer, device_id_type=MESH)

    loads = [
        pltpu.make_async_copy(src, dst, in_s.at[i])
        for i, (src, dst) in enumerate(((q_hbm, q_ref), (k_hbm, k_ref), (v_hbm, v_ref), (do_hbm, do_ref)))
    ]
    for load in loads:
        load.start()

    def w_rows(j):
        return pl.ds(pl.multiple_of(j * wr, wr), wr)

    def w_own(j):
        return pltpu.make_async_copy(w_hbm.at[:, w_rows(j), :], wbuf.at[j, :, c, x, z], own_s)

    for j in range(nc):
        w_own(j).start()

    owner, hashed = owner_ref[...], hash_ref[...]
    live = jnp.zeros_like(owner)
    for o in range(NX * NZ * CORES):
        live = jnp.where(owner == o, live_ref[o], live)
    high, blocks = hashed >> 7, live >> 7
    third = high - 3 * ((high * 21846) >> 16)
    high = jnp.where(blocks == 3, third, high & (blocks - 1))
    mbuf[c * NX + x, 0:3, :] = owner
    mbuf[c * NX + x, 3:6, :] = (hashed & 127) + high * 128
    mbuf[c * NX + x, 6:8, :] = jnp.zeros((2, tokens), I32)

    width = out_ref.shape[1]
    group = per_block * wr
    p = iota((LANES, width), 0)
    home = wr * nc * (CORES * ((p & (group - 1)) // wr) + p // group) + (p & (wr - 1))
    for j in range(nc):
        order[j] = jnp.where(home + wr * j == iota((LANES, width), 1), 1.0, 0.0).astype(BF16)
    upper[...] = jnp.where(iota((tokens, tokens), 0) < iota((tokens, tokens), 1), 1.0, 0.0).astype(BF16)

    pltpu.make_async_copy(w_hbm, w_hbm, own_s).wait()
    pl.semaphore_wait(barrier, len(peers))

    def wz(j, k):
        return copy(w_hbm.at[0:2, w_rows(j), :], wbuf.at[j, 0:2, c, x, z], wz_s.at[j], wz_r.at[j], at(x, z + k, c))

    def wx(j, k):
        return copy(w_hbm.at[2, w_rows(j), :], wbuf.at[j, 2, c, x, z], wx_s.at[j], wx_r.at[j], at(x + k, z, c))

    def wzx(j, k):
        ref = wbuf.at[j, 0:2, c, x]
        return copy(ref, ref, wzx_s.at[j], wzx_r.at[j], at(x + k, z, c))

    def wxz(j, k):
        ref = wbuf.at[j, 2, c, :, z]
        return copy(ref, ref, wxz_s.at[j], wxz_r.at[j], at(x, z + k, c))

    def wc(j, part):
        ref = wbuf.at[j, part, c]
        return copy(ref, ref, wc_s.at[j], wc_r.at[j], sibling)

    def meta_copy(i):
        dx, dc = plane[i]
        ref = mbuf.at[c * NX + x]
        return copy(ref, ref, m_s, m_r, at(x + dx, z, c + dc))

    def all_of(ref, ssem, rsem):
        return copy(ref, ref, ssem, rsem, sibling)

    def all_wz(j):
        return all_of(wbuf.at[j, 0:2, c, x, 0 : NZ - 1], wz_s.at[j], wz_r.at[j])

    def all_wx(j):
        return all_of(wbuf.at[j, 2, c, 0 : NX - 1, z], wx_s.at[j], wx_r.at[j])

    def all_wzx(j):
        return all_of(wbuf.at[j, 0:2, c, 0 : NX - 1], wzx_s.at[j], wzx_r.at[j])

    def all_wxz(j):
        return all_of(wbuf.at[j, 2, c, :, 0 : NZ - 1], wxz_s.at[j], wxz_r.at[j])

    def all_wc(j):
        return all_of(wbuf.at[j, :, c], wc_s.at[j], wc_r.at[j])

    all_meta = all_of(mbuf.at[0 : sources - 1], m_s, m_r)

    for k in x_far:
        wx(0, k).start()
    for k in z_far:
        wz(0, k).start()
    for i in range(len(plane)):
        meta_copy(i).start()
    for j in range(1, nc):
        for k in x_far:
            wx(j, k).start()

    def stage_wa(j):
        all_wz(j).wait_recv()
        for k in x_far:
            wzx(j, k).start()
        all_wz(j).wait_send()

    def stage_wx(j):
        all_wx(j).wait_recv()
        for k in z_far:
            wxz(j, k).start()

        @pl.when(j < nc - 1)
        def _():
            for k in z_far:
                wz(j + 1, k).start()

        all_wx(j).wait_send()

    def stage_wb(j):
        all_wzx(j).wait_recv()
        wc(j, slice(0, 2)).start()

    def stage_wc(j):
        all_wxz(j).wait_recv()
        wc(j, 2).start()

    def weights_ready(j):
        all_wc(j).wait_recv()
        all_wc(j).wait_send()
        all_wzx(j).wait_send()
        all_wxz(j).wait_send()

    entries = NZ * CAP
    deep = sources * CAP

    def stage_picks(_):
        mine = (x * NZ + iota((NZ, tokens), 0)) * CORES + c
        all_meta.wait_recv()

        def body(source, carry):
            part = mbuf.at[source]
            hits = [part[n : n + 1, :] == mine for n in range(3)]
            slot = jnp.zeros((NZ, tokens), I32)
            named = jnp.zeros((NZ, tokens), F32)
            for n in range(3):
                slot = jnp.where(hits[n], part[n + 3 : n + 4, :], slot)
                named = jnp.where(hits[n], 1.0, named)
            rank = nn(named.astype(BF16), upper[...])
            code = jnp.where(named > 0.5, rank, -1.0).astype(I32)
            for b in range(NZ):
                p1[source, b * CAP : (b + 1) * CAP, :] = jnp.where(
                    code[b : b + 1, :] == iota((CAP, tokens), 0), 1.0, 0.0
                ).astype(BF16)
            halves = jnp.concatenate([slot & 255, slot >> 8], axis=0).astype(F32).astype(BF16)
            moved = nt(halves, p1[source])
            own = iota((NZ, entries), 0) * CAP
            at_entry = iota((NZ, entries), 1)
            inside = (at_entry >= own) & (at_entry < own + CAP)
            cslot[0, pl.ds(source, 1), :] = jnp.sum(jnp.where(inside, moved[:NZ], 0.0), axis=0, keepdims=True)
            cslot[1, pl.ds(source, 1), :] = jnp.sum(jnp.where(inside, moved[NZ:], 0.0), axis=0, keepdims=True)
            return carry

        lax.fori_loop(0, sources, body, 0)
        all_meta.wait_send()

    def stage_slots(_):
        def body(b, carry):
            entry = iota((sources, deep), 1)
            first = iota((sources, deep), 0) * CAP
            inside = (entry >= first) & (entry < first + CAP)
            rank = entry[:1] - jnp.sum(jnp.where(entry >= first, CAP, 0), axis=0, keepdims=True) + CAP
            spread = jnp.where(iota((entries, deep), 0) == rank + b * CAP, 1.0, 0.0).astype(BF16)
            low = nn(cslot[0].astype(BF16), spread)
            top = nn(cslot[1].astype(BF16), spread)
            slot = jnp.sum(jnp.where(inside, low + 256.0 * top, 0.0), axis=0, keepdims=True).astype(I32)
            p2[b] = jnp.where(iota((SLOTS, deep), 0) == slot, 1.0, 0.0).astype(BF16)
            return carry

        lax.fori_loop(0, NZ, body, 0)

    def piece(h):
        return pl.ds(h * trows, trows)

    def tx(j, h, k):
        ref = tbuf.at[j, c, x, piece(h)]
        return copy(ref, ref, tx_s.at[j], tx_r.at[j, h], at(x + k, z, c))

    def tc(j, h):
        ref = tbuf.at[j, c, :, piece(h)]
        return copy(ref, ref, tc_s.at[j], tc_r.at[j], sibling)

    def all_tc(j):
        return all_of(tbuf.at[j, c], tc_s.at[j], tc_r.at[j])

    def y_partial(j, block):
        first = block * per_block
        x_, z_ = first // NZ, lax.rem(first, NZ)
        total = None
        for i in range(3):
            w = [wbuf[j, i, c_, x_, pl.ds(z_, per_block)].reshape(per_block * wr, -1) for c_ in range(CORES)]
            term = nt(grads[i], jnp.concatenate(w, axis=0))
            total = term if total is None else total + term
        return total

    def y_done(j, h, value):
        tbuf[j, c, x, piece(h), :] = value
        for k in x_far:
            tx(j, h, k).start()

    def stage_xb(j):
        for h in range(PIECES):
            all_of(tbuf.at[j, c, 0 : NX - 1, piece(h)], tx_s.at[j], tx_r.at[j, h]).wait_recv()
            tc(j, h).start()
        all_of(tbuf.at[j, c, 0 : NX - 1], tx_s.at[j], tx_r.at[j, 0]).wait_send()

    def stage_c(j):
        all_tc(j).wait_recv()

        def body(source, carry):
            picked = nn(p1[source], tbuf[j, source // NX, lax.rem(source, NX)]).astype(BF16)
            start = pl.multiple_of(source * CAP, CAP)
            for b in range(NZ):
                cbuf[j, b, pl.ds(start, CAP), :] = picked[b * CAP : (b + 1) * CAP]
            return carry

        lax.fori_loop(0, sources, body, 0)
        all_tc(j).wait_send()

    def z_partial(j, block):
        return nn(p2[block], cbuf[j, block])

    def z_done(j, h, value):
        size = SLOTS // PIECES
        tfin[j, pl.ds(h * size, size), :] = value

    ring_y = Ring(copy, y, NY, row(y - 1), row(y + 1), y_partial, y_done, ysend, yrecv, ys_s, ys_r)
    ring_z = Ring(copy, z, NZ, at(x, z - 1, c), at(x, z + 1, c), z_partial, z_done, zsend, zrecv, zs_s, zs_r)

    def stage_att(head):
        @pl.when(head == 0)
        def _():
            for load in loads:
                load.wait()

        for h in range(q_ref.shape[1] // HD):

            @pl.when(head == h)
            def _():
                attention(h, q_ref, k_ref, v_ref, do_ref, grads, dk_acc, dv_acc)

    def stage_y0(j):
        weights_ready(j)
        ring_y.step(0, j)

    runs = {
        "att": stage_att, "picks": stage_picks, "slots": stage_slots, "WA": stage_wa, "WX": stage_wx,
        "WB": stage_wb, "WC": stage_wc, "XB": stage_xb, "C": stage_c, "Y0": stage_y0,
    }
    for s in range(1, my + 1):
        runs["Y%d" % (s if s < my else 4)] = functools.partial(ring_y.step, s)
    for s in range(mz + 1):
        runs["Z%d" % (s if s < mz else 4)] = functools.partial(ring_z.step, s)

    words = []
    for first in range(0, len(ORDER), 4):
        words.append(sum(code << (7 * i) for i, code in enumerate(ORDER[first : first + 4])))

    def choose(stage, index, low, high):
        if high - low == 1:
            if NAMES[low] in runs:
                runs[NAMES[low]](index)
            return
        middle = (low + high) // 2

        @pl.when(stage < middle)
        def _():
            choose(stage, index, low, middle)

        @pl.when(stage >= middle)
        def _():
            choose(stage, index, middle, high)

    def iteration(t, carry):
        word = jnp.int32(0)
        for i, value in enumerate(words):
            word = jnp.where(t // 4 == i, value, word)
        place = lax.rem(t, 4)
        word = jnp.where(place >= 2, word // 16384, word)
        word = jnp.where(lax.rem(place, 2) == 1, word // 128, word)
        code = lax.rem(word, 128)
        choose(code // 4, lax.rem(code, 4), 0, len(NAMES))
        return carry

    lax.fori_loop(0, len(ORDER), iteration, 0)

    total = None
    for j in range(nc):
        term = nn(tfin[j], order[j])
        total = term if total is None else total + term
    out_ref[...] = total.astype(BF16)


def local(queries, key_rows, value_rows, out_grad, qkv_weight, row_owner, row_hash, live_rows):
    tokens, features = queries.shape
    shard = qkv_weight.shape[1]
    per_block = NX * NZ // NY
    wr = LANES // (CORES * per_block)
    nc = shard // wr
    my, mz = NY // 2, NZ // 2
    dma = lambda *shape: pltpu.SemaphoreType.DMA(shape)
    vmem, anywhere = pl.BlockSpec(memory_space=pltpu.VMEM), pl.BlockSpec(memory_space=pl.ANY)
    sources = CORES * NX
    both = lambda *shape: [dma(*shape), dma(*shape)]
    return pl.pallas_call(
        kernel,
        out_shape=jax.ShapeDtypeStruct((SLOTS, nc * LANES), BF16),
        in_specs=[anywhere] * 5 + [vmem] * 2 + [pl.BlockSpec(memory_space=pltpu.SMEM)],
        out_specs=vmem,
        scratch_shapes=[pltpu.VMEM((tokens, features), BF16)] * 4
        + [
            pltpu.VMEM((3, tokens, features), BF16),
            pltpu.VMEM((tokens, HD), F32),
            pltpu.VMEM((tokens, HD), F32),
            pltpu.VMEM((nc, 3, CORES, NX, NZ, wr, features), BF16),
            pltpu.VMEM((nc, CORES, NX, tokens, LANES), BF16),
            pltpu.VMEM((CORES * NX, 8, tokens), I32),
            pltpu.VMEM((nc, my, 2, tokens, LANES), BF16),
            pltpu.VMEM((nc, my, 2, tokens, LANES), BF16),
            pltpu.VMEM((nc, mz, 2, SLOTS, LANES), BF16),
            pltpu.VMEM((nc, mz, 2, SLOTS, LANES), BF16),
            pltpu.VMEM((tokens, tokens), BF16),
            pltpu.VMEM((sources, NZ * CAP, tokens), BF16),
            pltpu.VMEM((NZ, SLOTS, sources * CAP), BF16),
            pltpu.VMEM((2, sources, NZ * CAP), F32),
            pltpu.VMEM((nc, NZ, sources * CAP, LANES), BF16),
            pltpu.VMEM((nc, SLOTS, LANES), BF16),
            pltpu.VMEM((nc, LANES, nc * LANES), BF16),
            dma(4), pltpu.SemaphoreType.DMA,
            *both(nc), *both(nc), *both(nc), *both(nc), *both(nc),
            pltpu.SemaphoreType.DMA, pltpu.SemaphoreType.DMA,
            dma(nc), dma(nc, PIECES), *both(nc),
            dma(nc, PIECES), dma(nc, PIECES, my), dma(nc, PIECES), dma(nc, PIECES, mz),
        ],
        compiler_params=pltpu.CompilerParams(
            collective_id=0, has_side_effects=True, vmem_limit_bytes=60 * 1024 * 1024
        ),
    )(queries, key_rows, value_rows, out_grad, qkv_weight, row_owner.T, row_hash.T, live_rows)


def solution(mesh):
    return jax.shard_map(
        local,
        mesh=mesh,
        in_specs=(
            P("dp", "tensor"),
            P("dp", "tensor"),
            P("dp", "tensor"),
            P("dp", "tensor"),
            P(None, "dp", "tensor"),
            P("dp", None),
            P("dp", None),
            P(),
        ),
        out_specs=P("dp", "tensor"),
        check_vma=False,
    )
```

time: 293 us -> 119 us (0.41)
  waiting for transfers between devices: 171 us -> 0 us
  Pallas kernels: 0 us -> 117 us
  other arithmetic: 41.6 us -> 0 us
  local copies, waits for them, and re-layouts: 29.6 us -> 1.87 us
  matrix products: 20.6 us -> 0 us
  starting transfers between devices: 16.7 us -> 0 us
  between operations: 13.6 us -> 0.01 us
    pallas_call x0 -> x1, Pallas kernels: none -> 117 us  [local(): pl.pallas_call(kernel, out_shape=jax.ShapeDtypeStruct((SLOTS, nc * LANES)...]
    all_gather x1 -> x0, waiting for transfers between devices: 78 us -> none  [local(): whole_weight = lax.all_gather(qkv_weight, 'dp', axis=1, tiled=True)]
    all_to_all x2 -> x0, waiting for transfers between devices: 72.1 us -> none  [the longest x1 72.1 us: local(): lax.all_to_all(outgoing.reshape(owner_count, capacity, columns), 'dp', sp...]
    scatter-add x1 -> x0, other arithmetic: 19.9 us -> none  [local(): table = jnp.zeros((SLOTS, columns), jnp.float32).at[arrived_slots.reshape...]
    reduce_scatter x1 -> x0, waiting for transfers between devices: 19.8 us -> none  [local(): lax.psum_scatter(partial_value.astype(jnp.bfloat16), 'tensor', scatter_di...]
    dot_general x5 -> x0, matrix products: 18.3 us -> none  [the longest x1 7.85 us: local(): jnp.einsum('jtc,jrc->tr', grads, whole_weight, preferred_element_type=jnp...]
    another operation x2 -> x0, other arithmetic: 18.2 us -> none
    all_to_all x2 -> x0, starting transfers between devices: 16.7 us -> none  [the longest x1 11.1 us: local(): lax.all_to_all(outgoing.reshape(owner_count, capacity, columns), 'dp', sp...]
  transfers between devices with their start and end apart: 4 -> 0, of which waited for: 3 -> 0; matrix products, arithmetic and copies ran while one was open for 21% -> 0% of each run, Pallas kernels for 0% -> 0%
where the time goes in v2:
time: 119 us; the launch traced here: 118 us
  Pallas kernels  117 us (98%)
  local copies, waits for them, and re-layouts  1.87 us (2%)
    pallas_call x1, Pallas kernels, local(): pl.pallas_call(kernel, out_shape=jax.ShapeDtypeStruct((SLOTS, nc * LANES)...  117 us

profile of v2, /device:TPU:1, one launch (start us, length us, event | category | flops | bytes accessed | tf_op | source)
XLA Modules:
  0.0 118.4 jit_solution(12338329691401398943)
XLA Ops:
  0.0 116.5 %shard_map.82 = bf16[512,512]{1,0:T(8,128)(2,1)} custom-call(bf16[512,256]{1,0:T(8,128)(2,1)} %q_hbm.1, bf16[512,256]{1,0:T(8,128)(2,1)} %k_hbm.1, bf16[512,256]{1,0:T(8,128)(2,1)} %v_hbm.1, bf16[512,256]{1,0:T(8,128)(2,1)} %do_hbm.1, bf16[3,64,256]{2,1,0:T(8,128)(2,1)} %w_hbm.1, s32[3,512]{1,0:T(4,128)} %bitcast.2, s32[3,512]{1,0:T(4,128)} %bitcast.3, ...), custom_call_target="tpu_custom_call" | custom-call | tf_op jit(solution)/shard_map/pallas_call | solution.py:480
  116.5 1.9 %copy.10 = bf16[512,512]{1,0:T(8,128)(2,1)} copy(bf16[512,512]{1,0:T(8,128)(2,1)} %shard_map.82) | data formatting | bytes 1048576

commit v3 on v2

--- a/solution.py
+++ b/solution.py
@@ -16,12 +16,12 @@
 SLOTS = 512
 CAP = 48
 PIECES = 2
-NAMES = ("Y0", "Y1", "Y2", "Y3", "Y4", "XB", "C", "Z0", "Z1", "Z2", "Z3", "Z4", "WA", "WX", "WB", "WC", "att", "picks", "slots")
+NAMES = ("Y0", "Y1", "Y2", "Y3", "Y4", "XB", "C", "Z0", "Z1", "Z2", "Z3", "Z4", "WA", "WX", "WY", "WB", "WC", "att", "picks", "slots")
 ORDER = (
-    52, 64, 48, 65, 53, 68, 60, 56, 49, 54, 0, 72, 4, 61, 50, 57, 55, 1, 8, 5,
-    62, 51, 58, 12, 2, 9, 16, 6, 63, 59, 13, 3, 10, 20, 17, 7, 24, 28, 14, 11,
-    21, 32, 25, 18, 29, 15, 36, 33, 19, 22, 37, 40, 26, 23, 30, 41, 27, 31, 34, 44,
-    35, 38, 45, 39, 42, 43, 46, 47,
+    68, 52, 69, 48, 72, 56, 49, 53, 76, 50, 60, 64, 57, 54, 55, 0, 51, 61, 4, 65,
+    1, 59, 8, 58, 5, 62, 12, 63, 67, 9, 66, 3, 2, 16, 13, 7, 6, 17, 20, 11,
+    24, 10, 21, 28, 15, 25, 29, 32, 14, 19, 33, 36, 18, 37, 23, 40, 27, 31, 22, 41,
+    26, 30, 35, 34, 39, 38, 43, 42, 47, 44, 45, 46,
 )
 
 
@@ -134,10 +134,10 @@
 
 
 def kernel(
-    q_hbm, k_hbm, v_hbm, do_hbm, w_hbm, owner_ref, hash_ref, live_ref, out_ref,
-    q_ref, k_ref, v_ref, do_ref, grads, dk_acc, dv_acc, wbuf, tbuf, mbuf, ysend, yrecv, zsend, zrecv,
+    q_hbm, k_hbm, v_hbm, do_hbm, w_hbm, owner_hbm, hash_hbm, live_hbm, out_ref,
+    q_ref, k_ref, v_ref, do_ref, owner_ref, hash_ref, live_ref, grads, dk_acc, dv_acc, wbuf, tbuf, mbuf, ysend, yrecv, zsend, zrecv,
     upper, p1, p2, cslot, cbuf, tfin, order,
-    in_s, own_s, wz_s, wz_r, wx_s, wx_r, wzx_s, wzx_r, wxz_s, wxz_r, wc_s, wc_r,
+    in_s, own_s, wz_s, wz_r, wx_s, wx_r, wzx_s, wzx_r, wxz_s, wxz_r, wxy_s, wxy_r, wc_s, wc_r,
     m_s, m_r, tx_s, tx_r, tc_s, tc_r, ys_s, ys_r, zs_s, zs_r,
 ):
     tokens = q_ref.shape[0]
@@ -163,7 +163,9 @@
 
     sibling = at(x, z, c + 1)
     plane = [(dx, dc) for dx in range(NX) for dc in range(CORES) if (dx, dc) != (0, 0)]
+    relayed = NZ == 8
     z_far = sorted(range(1, NZ), key=lambda k: -min(k, NZ - k))
+    z_near = (1, NZ - 1, 2, NZ - 2) if relayed else z_far
     x_far = sorted(range(1, NX), key=lambda k: -min(k, NX - k))
 
     barrier = pltpu.get_barrier_semaphore()
@@ -177,7 +179,11 @@
         pltpu.make_async_copy(src, dst, in_s.at[i])
         for i, (src, dst) in enumerate(((q_hbm, q_ref), (k_hbm, k_ref), (v_hbm, v_ref), (do_hbm, do_ref)))
     ]
-    for load in loads:
+    tables = [
+        pltpu.make_async_copy(src, dst, in_s.at[4 + i])
+        for i, (src, dst) in enumerate(((owner_hbm, owner_ref), (hash_hbm, hash_ref), (live_hbm, live_ref)))
+    ]
+    for load in tables + loads:
         load.start()
 
     def w_rows(j):
@@ -189,6 +195,71 @@
     for j in range(nc):
         w_own(j).start()
 
+    pl.semaphore_wait(barrier, len(peers))
+
+    def wz(j, k):
+        return copy(w_hbm.at[0:2, w_rows(j), :], wbuf.at[j, 0:2, c, x, z], wz_s.at[j], wz_r.at[j], at(x, z + k, c))
+
+    def wx(j, k):
+        return copy(w_hbm.at[2, w_rows(j), :], wbuf.at[j, 2, c, x, z], wx_s.at[j], wx_r.at[j], at(x + k, z, c))
+
+    def wzx(j, k):
+        ref = wbuf.at[j, 0:2, c, x]
+        return copy(ref, ref, wzx_s.at[j], wzx_r.at[j], at(x + k, z, c))
+
+    def wxz(j, k):
+        ref = wbuf.at[j, 2, c, :, z]
+        return copy(ref, ref, wxz_s.at[j], wxz_r.at[j], at(x, z + k, c))
+
+    def wxy(j, k, half):
+        origin = lax.rem(z + NZ - 2 if k > 0 else z + 2, NZ)
+        ref = wbuf.at[j, 2, c, :, origin] if half is None else wbuf.at[j, 2, c, half, origin]
+        return copy(ref, ref, wxy_s.at[j], wxy_r.at[j], at(x, z + k, c))
+
+    def wc(j, part):
+        ref = wbuf.at[j, part, c]
+        return copy(ref, ref, wc_s.at[j], wc_r.at[j], sibling)
+
+    def meta_copy(i):
+        dx, dc = plane[i]
+        ref = mbuf.at[c * NX + x]
+        return copy(ref, ref, m_s, m_r, at(x + dx, z, c + dc))
+
+    def all_of(ref, ssem, rsem):
+        return copy(ref, ref, ssem, rsem, sibling)
+
+    def all_wz(j):
+        return all_of(wbuf.at[j, 0:2, c, x, 0 : NZ - 1], wz_s.at[j], wz_r.at[j])
+
+    def all_wx(j):
+        return all_of(wbuf.at[j, 2, c, 0 : NX - 1, z], wx_s.at[j], wx_r.at[j])
+
+    def all_wzx(j):
+        return all_of(wbuf.at[j, 0:2, c, 0 : NX - 1], wzx_s.at[j], wzx_r.at[j])
+
+    def all_wxz(j):
+        return all_of(wbuf.at[j, 2, c, :, 0 : len(z_near)], wxz_s.at[j], wxz_r.at[j])
+
+    def all_wxy(j):
+        return all_of(wbuf.at[j, 2, c, :, 0:3], wxy_s.at[j], wxy_r.at[j])
+
+    def all_wc(j):
+        return all_of(wbuf.at[j, :, c], wc_s.at[j], wc_r.at[j])
+
+    all_meta = all_of(mbuf.at[0 : sources - 1], m_s, m_r)
+
+    for k in x_far:
+        wx(0, k).start()
+    for k in z_far:
+        wz(0, k).start()
+    for j in range(1, nc):
+        for k in x_far:
+            wx(j, k).start()
+    for k in z_far:
+        wz(1, k).start()
+
+    for load in tables:
+        load.wait()
     owner, hashed = owner_ref[...], hash_ref[...]
     live = jnp.zeros_like(owner)
     for o in range(NX * NZ * CORES):
@@ -199,7 +270,8 @@
     mbuf[c * NX + x, 0:3, :] = owner
     mbuf[c * NX + x, 3:6, :] = (hashed & 127) + high * 128
     mbuf[c * NX + x, 6:8, :] = jnp.zeros((2, tokens), I32)
-
+    for i in range(len(plane)):
+        meta_copy(i).start()
     width = out_ref.shape[1]
     group = per_block * wr
     p = iota((LANES, width), 0)
@@ -207,62 +279,7 @@
     for j in range(nc):
         order[j] = jnp.where(home + wr * j == iota((LANES, width), 1), 1.0, 0.0).astype(BF16)
     upper[...] = jnp.where(iota((tokens, tokens), 0) < iota((tokens, tokens), 1), 1.0, 0.0).astype(BF16)
-
     pltpu.make_async_copy(w_hbm, w_hbm, own_s).wait()
-    pl.semaphore_wait(barrier, len(peers))
-
-    def wz(j, k):
-        return copy(w_hbm.at[0:2, w_rows(j), :], wbuf.at[j, 0:2, c, x, z], wz_s.at[j], wz_r.at[j], at(x, z + k, c))
-
-    def wx(j, k):
-        return copy(w_hbm.at[2, w_rows(j), :], wbuf.at[j, 2, c, x, z], wx_s.at[j], wx_r.at[j], at(x + k, z, c))
-
-    def wzx(j, k):
-        ref = wbuf.at[j, 0:2, c, x]
-        return copy(ref, ref, wzx_s.at[j], wzx_r.at[j], at(x + k, z, c))
-
-    def wxz(j, k):
-        ref = wbuf.at[j, 2, c, :, z]
-        return copy(ref, ref, wxz_s.at[j], wxz_r.at[j], at(x, z + k, c))
-
-    def wc(j, part):
-        ref = wbuf.at[j, part, c]
-        return copy(ref, ref, wc_s.at[j], wc_r.at[j], sibling)
-
-    def meta_copy(i):
-        dx, dc = plane[i]
-        ref = mbuf.at[c * NX + x]
-        return copy(ref, ref, m_s, m_r, at(x + dx, z, c + dc))
-
-    def all_of(ref, ssem, rsem):
-        return copy(ref, ref, ssem, rsem, sibling)
-
-    def all_wz(j):
-        return all_of(wbuf.at[j, 0:2, c, x, 0 : NZ - 1], wz_s.at[j], wz_r.at[j])
-
-    def all_wx(j):
-        return all_of(wbuf.at[j, 2, c, 0 : NX - 1, z], wx_s.at[j], wx_r.at[j])
-
-    def all_wzx(j):
-        return all_of(wbuf.at[j, 0:2, c, 0 : NX - 1], wzx_s.at[j], wzx_r.at[j])
-
-    def all_wxz(j):
-        return all_of(wbuf.at[j, 2, c, :, 0 : NZ - 1], wxz_s.at[j], wxz_r.at[j])
-
-    def all_wc(j):
-        return all_of(wbuf.at[j, :, c], wc_s.at[j], wc_r.at[j])
-
-    all_meta = all_of(mbuf.at[0 : sources - 1], m_s, m_r)
-
-    for k in x_far:
-        wx(0, k).start()
-    for k in z_far:
-        wz(0, k).start()
-    for i in range(len(plane)):
-        meta_copy(i).start()
-    for j in range(1, nc):
-        for k in x_far:
-            wx(j, k).start()
 
     def stage_wa(j):
         all_wz(j).wait_recv()
@@ -272,22 +289,30 @@
 
     def stage_wx(j):
         all_wx(j).wait_recv()
-        for k in z_far:
+        for k in z_near:
             wxz(j, k).start()
 
-        @pl.when(j < nc - 1)
+        @pl.when(j < nc - 2)
         def _():
             for k in z_far:
-                wz(j + 1, k).start()
+                wz(j + 2, k).start()
 
         all_wx(j).wait_send()
+
+    def stage_wy(j):
+        all_wxz(j).wait_recv()
+        if relayed:
+            for side, step in enumerate((1, -1)):
+                wxy(j, 2 * step, pl.ds(side * (NX // 2), NX // 2)).start()
+                wxy(j, step, None).start()
 
     def stage_wb(j):
         all_wzx(j).wait_recv()
         wc(j, slice(0, 2)).start()
 
     def stage_wc(j):
-        all_wxz(j).wait_recv()
+        if relayed:
+            all_wxy(j).wait_recv()
         wc(j, 2).start()
 
     def weights_ready(j):
@@ -295,6 +320,8 @@
         all_wc(j).wait_send()
         all_wzx(j).wait_send()
         all_wxz(j).wait_send()
+        if relayed:
+            all_wxy(j).wait_send()
 
     entries = NZ * CAP
     deep = sources * CAP
@@ -389,7 +416,7 @@
                 cbuf[j, b, pl.ds(start, CAP), :] = picked[b * CAP : (b + 1) * CAP]
             return carry
 
-        lax.fori_loop(0, sources, body, 0)
+        lax.fori_loop(0, sources, body, 0, unroll=2)
         all_tc(j).wait_send()
 
     def z_partial(j, block):
@@ -420,7 +447,7 @@
 
     runs = {
         "att": stage_att, "picks": stage_picks, "slots": stage_slots, "WA": stage_wa, "WX": stage_wx,
-        "WB": stage_wb, "WC": stage_wc, "XB": stage_xb, "C": stage_c, "Y0": stage_y0,
+        "WY": stage_wy, "WB": stage_wb, "WC": stage_wc, "XB": stage_xb, "C": stage_c, "Y0": stage_y0,
     }
     for s in range(1, my + 1):
         runs["Y%d" % (s if s < my else 4)] = functools.partial(ring_y.step, s)
@@ -480,9 +507,11 @@
     return pl.pallas_call(
         kernel,
         out_shape=jax.ShapeDtypeStruct((SLOTS, nc * LANES), BF16),
-        in_specs=[anywhere] * 5 + [vmem] * 2 + [pl.BlockSpec(memory_space=pltpu.SMEM)],
+        in_specs=[anywhere] * 8,
         out_specs=vmem,
         scratch_shapes=[pltpu.VMEM((tokens, features), BF16)] * 4
+        + [pltpu.VMEM((3, tokens), I32)] * 2
+        + [pltpu.SMEM(live_rows.shape, I32)]
         + [
             pltpu.VMEM((3, tokens, features), BF16),
             pltpu.VMEM((tokens, HD), F32),
@@ -501,8 +530,8 @@
             pltpu.VMEM((nc, NZ, sources * CAP, LANES), BF16),
             pltpu.VMEM((nc, SLOTS, LANES), BF16),
             pltpu.VMEM((nc, LANES, nc * LANES), BF16),
-            dma(4), pltpu.SemaphoreType.DMA,
-            *both(nc), *both(nc), *both(nc), *both(nc), *both(nc),
+            dma(7), pltpu.SemaphoreType.DMA,
+            *both(nc), *both(nc), *both(nc), *both(nc), *both(nc), *both(nc),
             pltpu.SemaphoreType.DMA, pltpu.SemaphoreType.DMA,
             dma(nc), dma(nc, PIECES), *both(nc),
             dma(nc, PIECES), dma(nc, PIECES, my), dma(nc, PIECES), dma(nc, PIECES, mz),

time: 119 us -> 117 us (0.983)
  Pallas kernels: 117 us -> 115 us
    pallas_call x1, Pallas kernels: 117 us -> 115 us  [local(): pl.pallas_call(kernel, out_shape=jax.ShapeDtypeStruct((SLOTS, nc * LANES)...]
where the time goes in v3:
time: 117 us; the launch traced here: 116 us
  Pallas kernels  115 us (98%)
  local copies, waits for them, and re-layouts  1.87 us (2%)
    pallas_call x1, Pallas kernels, local(): pl.pallas_call(kernel, out_shape=jax.ShapeDtypeStruct((SLOTS, nc * LANES)...  115 us

profile of v3, /device:TPU:1, one launch (start us, length us, event | category | flops | bytes accessed | tf_op | source)
XLA Modules:
  0.0 116.4 jit_solution(9818462724067850727)
XLA Ops:
  0.0 114.5 %shard_map.82 = bf16[512,512]{1,0:T(8,128)(2,1)} custom-call(bf16[512,256]{1,0:T(8,128)(2,1)} %q_hbm.1, bf16[512,256]{1,0:T(8,128)(2,1)} %k_hbm.1, bf16[512,256]{1,0:T(8,128)(2,1)} %v_hbm.1, bf16[512,256]{1,0:T(8,128)(2,1)} %do_hbm.1, bf16[3,64,256]{2,1,0:T(8,128)(2,1)} %w_hbm.1, s32[3,512]{1,0:T(4,128)} %bitcast.2, s32[3,512]{1,0:T(4,128)} %bitcast.3, ...), custom_call_target="tpu_custom_call" | custom-call | tf_op jit(solution)/shard_map/pallas_call | solution.py:507
  114.5 1.9 %copy.10 = bf16[512,512]{1,0:T(8,128)(2,1)} copy(bf16[512,512]{1,0:T(8,128)(2,1)} %shard_map.82) | data formatting | bytes 1048576

commit v4 on v3

--- a/solution.py
+++ b/solution.py
@@ -16,12 +16,12 @@
 SLOTS = 512
 CAP = 48
 PIECES = 2
-NAMES = ("Y0", "Y1", "Y2", "Y3", "Y4", "XB", "C", "Z0", "Z1", "Z2", "Z3", "Z4", "WA", "WX", "WY", "WB", "WC", "att", "picks", "slots")
+NAMES = ("A0", "A1", "A2", "B0", "B1", "B2", "Y0", "Y1", "Y2", "Y3", "Y4", "XB", "C", "Z0", "Z1", "Z2", "Z3", "Z4", "WA", "WX", "WY", "WB", "WC", "att", "picks", "slots")
 ORDER = (
-    68, 52, 69, 48, 72, 56, 49, 53, 76, 50, 60, 64, 57, 54, 55, 0, 51, 61, 4, 65,
-    1, 59, 8, 58, 5, 62, 12, 63, 67, 9, 66, 3, 2, 16, 13, 7, 6, 17, 20, 11,
-    24, 10, 21, 28, 15, 25, 29, 32, 14, 19, 33, 36, 18, 37, 23, 40, 27, 31, 22, 41,
-    26, 30, 35, 34, 39, 38, 43, 42, 47, 44, 45, 46,
+    92, 76, 93, 72, 96, 80, 77, 73, 100, 84, 81, 78, 88, 79, 0, 4, 85, 74, 75, 89,
+    25, 82, 8, 83, 29, 36, 86, 90, 33, 26, 91, 40, 37, 87, 30, 27, 41, 44, 34, 31,
+    48, 38, 45, 12, 16, 35, 49, 13, 42, 39, 17, 20, 43, 21, 46, 64, 50, 47, 54, 65,
+    51, 55, 58, 59, 69, 62, 63, 68, 66, 67, 70, 71,
 )
 
 
@@ -70,9 +70,9 @@
 
 
 class Ring:
-    def __init__(self, copy, me, n, left, right, partial, done, out, inc, ss, rs):
+    def __init__(self, copy, me, n, to, skip_to, partial, done, out, inc, ss, rs):
         self.copy, self.me, self.n, self.m = copy, me, n, n // 2
-        self.to, self.partial, self.done = (left, right), partial, done
+        self.to, self.skip_to, self.partial, self.done = to, skip_to, partial, done
         self.out, self.inc, self.ss, self.rs = out, inc, ss, rs
         self.size = out.shape[3] // PIECES
 
@@ -81,10 +81,11 @@
             return h * self.size, self.size
         return h * self.size + side * (self.size // 2), self.size // 2
 
-    def hop(self, j, s, h, side):
+    def hop(self, j, s, h, side, skip=False):
         part = pl.ds(*self.rows(h, side if s == 0 else None))
+        where = self.skip_to[side] if skip and s == 0 else self.to[side]
         return self.copy(
-            self.out.at[j, s, side, part], self.inc.at[j, s, side, part], self.ss.at[j, h], self.rs.at[j, h, s], self.to[side]
+            self.out.at[j, s, side, part], self.inc.at[j, s, side, part], self.ss.at[j, h], self.rs.at[j, h, s], where
         )
 
     def both(self, j, s, h):
@@ -92,7 +93,11 @@
         ref = self.inc.at[j, 0, 0, part] if s == 0 else self.inc.at[j, s, :, part]
         return self.copy(ref, ref, self.ss.at[j, h], self.rs.at[j, h, s], self.to[0])
 
-    def step(self, s, j):
+    def sent_early(self, j, h):
+        ref = self.out.at[j, 0:3, 0, pl.ds(*self.rows(h))]
+        return self.copy(ref, ref, self.ss.at[j, h], self.rs.at[j, h, 0], self.to[0])
+
+    def step(self, s, j, skip=False):
         m, n, out, inc = self.m, self.n, self.out, self.inc
         if s == 0:
             value = self.partial(j, lax.rem(self.me + m, n)).astype(BF16)
@@ -100,7 +105,7 @@
                 for side in range(2):
                     start, count = self.rows(h, side)
                     out[j, 0, side, start : start + count, :] = value[start : start + count]
-                    self.hop(j, 0, h, side).start()
+                    self.hop(j, 0, h, side, skip).start()
             return
         if s < m:
             values = [
@@ -110,8 +115,18 @@
         else:
             values = [self.partial(j, self.me)]
         for h in range(PIECES):
+            if skip and s == 1:
+                for side, value in enumerate(values):
+                    start, count = self.rows(h)
+                    out[j, 1, side, start : start + count, :] = value[start : start + count]
+                    self.hop(j, 1, h, side).start()
+                continue
             self.both(j, s - 1, h).wait_recv()
-            self.both(j, s - 1, h).wait_send()
+            if skip and s == 2:
+                self.both(j, 0, h).wait_recv()
+                self.sent_early(j, h).wait_send()
+            else:
+                self.both(j, s - 1, h).wait_send()
             start, count = self.rows(h)
             whole = slice(start, start + count)
             halves = [slice(first, first + size) for first, size in (self.rows(h, 0), self.rows(h, 1))]
@@ -128,6 +143,10 @@
                     near, far = halves[side], halves[1 - side]
                     out[j, s, side, near, :] = value[near] + inc[j, 0, side, near, :]
                     out[j, s, side, far, :] = value[far]
+                elif skip and s == 2:
+                    near, far = halves[side], halves[1 - side]
+                    out[j, s, side, near, :] = value[near] + inc[j, 1, side, near, :] + inc[j, 0, side, near, :]
+                    out[j, s, side, far, :] = value[far] + inc[j, 1, side, far, :]
                 else:
                     out[j, s, side, whole, :] = value[whole] + inc[j, s - 1, side, whole, :]
                 self.hop(j, s, h, side).start()
@@ -172,6 +191,8 @@
     peers = [at(x, z + k, c) for k in z_far]
     peers += [at(x + dx, z, c + dc) for dx, dc in plane]
     peers += [row(y + 1), row(y - 1)]
+    if NY > 4:
+        peers += [row(y + 2), row(y + NY - 2)]
     for peer in peers:
         pl.semaphore_signal(barrier, inc=1, device_id=peer, device_id_type=MESH)
 
@@ -426,8 +447,13 @@
         size = SLOTS // PIECES
         tfin[j, pl.ds(h * size, size), :] = value
 
-    ring_y = Ring(copy, y, NY, row(y - 1), row(y + 1), y_partial, y_done, ysend, yrecv, ys_s, ys_r)
-    ring_z = Ring(copy, z, NZ, at(x, z - 1, c), at(x, z + 1, c), z_partial, z_done, zsend, zrecv, zs_s, zs_r)
+    ring_y = Ring(
+        copy, y, NY, (row(y - 1), row(y + 1)), (row(y + NY - 2), row(y + 2)), y_partial, y_done, ysend, yrecv, ys_s, ys_r
+    )
+    ring_z = Ring(
+        copy, z, NZ, (at(x, z - 1, c), at(x, z + 1, c)), (at(x, z + NZ - 2, c), at(x, z + 2, c)),
+        z_partial, z_done, zsend, zrecv, zs_s, zs_r,
+    )
 
     def stage_att(head):
         @pl.when(head == 0)
@@ -441,9 +467,9 @@
             def _():
                 attention(h, q_ref, k_ref, v_ref, do_ref, grads, dk_acc, dv_acc)
 
-    def stage_y0(j):
+    def stage_y0(j, skip=False):
         weights_ready(j)
-        ring_y.step(0, j)
+        ring_y.step(0, j, skip)
 
     runs = {
         "att": stage_att, "picks": stage_picks, "slots": stage_slots, "WA": stage_wa, "WX": stage_wx,
@@ -451,6 +477,12 @@
     }
     for s in range(1, my + 1):
         runs["Y%d" % (s if s < my else 4)] = functools.partial(ring_y.step, s)
+    if my == 4 and mz == 4:
+        runs["A0"] = functools.partial(stage_y0, skip=True)
+        for s in range(3):
+            runs["B%d" % s] = functools.partial(ring_z.step, s, skip=True)
+            if s > 0:
+                runs["A%d" % s] = functools.partial(ring_y.step, s, skip=True)
     for s in range(mz + 1):
         runs["Z%d" % (s if s < mz else 4)] = functools.partial(ring_z.step, s)
 

time: 117 us -> 116 us (level)
  no operation moved by 1% of the time
where the time goes in v4:
time: 116 us
  Pallas kernels  114 us (98%)
  local copies, waits for them, and re-layouts  1.87 us (2%)
    pallas_call x1, Pallas kernels, local(): pl.pallas_call(kernel, out_shape=jax.ShapeDtypeStruct((SLOTS, nc * LANES)...  114 us

profile of v4, /device:TPU:1, one launch (start us, length us, event | category | flops | bytes accessed | tf_op | source)
XLA Modules:
  0.0 115.5 jit_solution(4809845528698019334)
XLA Ops:
  0.0 113.6 %shard_map.82 = bf16[512,512]{1,0:T(8,128)(2,1)} custom-call(bf16[512,256]{1,0:T(8,128)(2,1)} %q_hbm.1, bf16[512,256]{1,0:T(8,128)(2,1)} %k_hbm.1, bf16[512,256]{1,0:T(8,128)(2,1)} %v_hbm.1, bf16[512,256]{1,0:T(8,128)(2,1)} %do_hbm.1, bf16[3,64,256]{2,1,0:T(8,128)(2,1)} %w_hbm.1, s32[3,512]{1,0:T(4,128)} %bitcast.2, s32[3,512]{1,0:T(4,128)} %bitcast.3, ...), custom_call_target="tpu_custom_call" | custom-call | tf_op jit(solution)/shard_map/pallas_call | solution.py:539
  113.7 1.9 %copy.10 = bf16[512,512]{1,0:T(8,128)(2,1)} copy(bf16[512,512]{1,0:T(8,128)(2,1)} %shard_map.82) | data formatting | bytes 1048576

commit v5 on v4

--- a/solution.py
+++ b/solution.py
@@ -18,10 +18,10 @@
 PIECES = 2
 NAMES = ("A0", "A1", "A2", "B0", "B1", "B2", "Y0", "Y1", "Y2", "Y3", "Y4", "XB", "C", "Z0", "Z1", "Z2", "Z3", "Z4", "WA", "WX", "WY", "WB", "WC", "att", "picks", "slots")
 ORDER = (
-    92, 76, 93, 72, 96, 80, 77, 73, 100, 84, 81, 78, 88, 79, 0, 4, 85, 74, 75, 89,
-    25, 82, 8, 83, 29, 36, 86, 90, 33, 26, 91, 40, 37, 87, 30, 27, 41, 44, 34, 31,
-    48, 38, 45, 12, 16, 35, 49, 13, 42, 39, 17, 20, 43, 21, 46, 64, 50, 47, 54, 65,
-    51, 55, 58, 59, 69, 62, 63, 68, 66, 67, 70, 71,
+    92, 76, 93, 72, 96, 80, 73, 77, 100, 84, 81, 88, 0, 74, 78, 4, 79, 75, 85, 89,
+    25, 82, 8, 29, 83, 36, 90, 86, 33, 26, 40, 91, 37, 87, 30, 27, 41, 44, 34, 31,
+    48, 12, 38, 45, 16, 35, 49, 13, 42, 17, 39, 20, 43, 21, 46, 64, 50, 54, 47, 65,
+    51, 55, 58, 59, 62, 63, 68, 66, 69, 67, 70, 71,
 )
 
 
@@ -437,7 +437,7 @@
                 cbuf[j, b, pl.ds(start, CAP), :] = picked[b * CAP : (b + 1) * CAP]
             return carry
 
-        lax.fori_loop(0, sources, body, 0, unroll=2)
+        lax.fori_loop(0, sources, body, 0, unroll=4)
         all_tc(j).wait_send()
 
     def z_partial(j, block):
@@ -516,13 +516,16 @@
         choose(code // 4, lax.rem(code, 4), 0, len(NAMES))
         return carry
 
-    lax.fori_loop(0, len(ORDER), iteration, 0)
-
+    lax.fori_loop(0, len(ORDER) - 1, iteration, 0)
+
+    last = ORDER[-1] % 4
     total = None
     for j in range(nc):
-        term = nn(tfin[j], order[j])
-        total = term if total is None else total + term
-    out_ref[...] = total.astype(BF16)
+        if j != last:
+            term = nn(tfin[j], order[j])
+            total = term if total is None else total + term
+    runs["Z4"](last)
+    out_ref[...] = (total + nn(tfin[last], order[last])).astype(BF16)
 
 
 def local(queries, key_rows, value_rows, out_grad, qkv_weight, row_owner, row_hash, live_rows):

time: 116 us -> 115 us (level)
  no operation moved by 1% of the time
where the time goes in v5:
time: 115 us; the launch traced here: 114 us
  Pallas kernels  113 us (98%)
  local copies, waits for them, and re-layouts  1.87 us (2%)
    pallas_call x1, Pallas kernels, local(): pl.pallas_call(kernel, out_shape=jax.ShapeDtypeStruct((SLOTS, nc * LANES)...  113 us

profile of v5, /device:TPU:1, one launch (start us, length us, event | category | flops | bytes accessed | tf_op | source)
XLA Modules:
  0.0 114.4 jit_solution(17334106810812462656)
XLA Ops:
  0.0 112.6 %shard_map.82 = bf16[512,512]{1,0:T(8,128)(2,1)} custom-call(bf16[512,256]{1,0:T(8,128)(2,1)} %q_hbm.1, bf16[512,256]{1,0:T(8,128)(2,1)} %k_hbm.1, bf16[512,256]{1,0:T(8,128)(2,1)} %v_hbm.1, bf16[512,256]{1,0:T(8,128)(2,1)} %do_hbm.1, bf16[3,64,256]{2,1,0:T(8,128)(2,1)} %w_hbm.1, s32[3,512]{1,0:T(4,128)} %bitcast.2, s32[3,512]{1,0:T(4,128)} %bitcast.3, ...), custom_call_target="tpu_custom_call" | custom-call | tf_op jit(solution)/shard_map/pallas_call | solution.py:542
  112.6 1.9 %copy.10 = bf16[512,512]{1,0:T(8,128)(2,1)} copy(bf16[512,512]{1,0:T(8,128)(2,1)} %shard_map.82) | data formatting | bytes 1048576

commit v6 on v5

--- a/solution.py
+++ b/solution.py
@@ -237,8 +237,7 @@
         ref = wbuf.at[j, 2, c, :, origin] if half is None else wbuf.at[j, 2, c, half, origin]
         return copy(ref, ref, wxy_s.at[j], wxy_r.at[j], at(x, z + k, c))
 
-    def wc(j, part):
-        ref = wbuf.at[j, part, c]
+    def wc(j, ref):
         return copy(ref, ref, wc_s.at[j], wc_r.at[j], sibling)
 
     def meta_copy(i):
@@ -306,6 +305,7 @@
         all_wz(j).wait_recv()
         for k in x_far:
             wzx(j, k).start()
+        wc(j, wbuf.at[j, 0:2, c, x]).start()
         all_wz(j).wait_send()
 
     def stage_wx(j):
@@ -329,12 +329,13 @@
 
     def stage_wb(j):
         all_wzx(j).wait_recv()
-        wc(j, slice(0, 2)).start()
+        for k in range(1, NX):
+            wc(j, wbuf.at[j, 0:2, c, lax.rem(x + k, NX)]).start()
 
     def stage_wc(j):
         if relayed:
             all_wxy(j).wait_recv()
-        wc(j, 2).start()
+        wc(j, wbuf.at[j, 2, c]).start()
 
     def weights_ready(j):
         all_wc(j).wait_recv()
@@ -399,8 +400,8 @@
         ref = tbuf.at[j, c, x, piece(h)]
         return copy(ref, ref, tx_s.at[j], tx_r.at[j, h], at(x + k, z, c))
 
-    def tc(j, h):
-        ref = tbuf.at[j, c, :, piece(h)]
+    def tc(j, h, k):
+        ref = tbuf.at[j, c, lax.rem(x + k, NX), piece(h)]
         return copy(ref, ref, tc_s.at[j], tc_r.at[j], sibling)
 
     def all_tc(j):
@@ -420,11 +421,13 @@
         tbuf[j, c, x, piece(h), :] = value
         for k in x_far:
             tx(j, h, k).start()
+        tc(j, h, 0).start()
 
     def stage_xb(j):
         for h in range(PIECES):
             all_of(tbuf.at[j, c, 0 : NX - 1, piece(h)], tx_s.at[j], tx_r.at[j, h]).wait_recv()
-            tc(j, h).start()
+            for k in range(1, NX):
+                tc(j, h, k).start()
         all_of(tbuf.at[j, c, 0 : NX - 1], tx_s.at[j], tx_r.at[j, 0]).wait_send()
 
     def stage_c(j):
@@ -437,7 +440,7 @@
                 cbuf[j, b, pl.ds(start, CAP), :] = picked[b * CAP : (b + 1) * CAP]
             return carry
 
-        lax.fori_loop(0, sources, body, 0, unroll=4)
+        lax.fori_loop(0, sources, body, 0, unroll=8)
         all_tc(j).wait_send()
 
     def z_partial(j, block):

time: 115 us -> 114 us (level)
  no operation moved by 1% of the time
where the time goes in v6:
time: 114 us
  Pallas kernels  112 us (98%)
  local copies, waits for them, and re-layouts  1.87 us (2%)
    pallas_call x1, Pallas kernels, local(): pl.pallas_call(kernel, out_shape=jax.ShapeDtypeStruct((SLOTS, nc * LANES)...  112 us

profile of v6, /device:TPU:1, one launch (start us, length us, event | category | flops | bytes accessed | tf_op | source)
XLA Modules:
  0.0 113.9 jit_solution(7478360938837221329)
XLA Ops:
  0.0 112.0 %shard_map.82 = bf16[512,512]{1,0:T(8,128)(2,1)} custom-call(bf16[512,256]{1,0:T(8,128)(2,1)} %q_hbm.1, bf16[512,256]{1,0:T(8,128)(2,1)} %k_hbm.1, bf16[512,256]{1,0:T(8,128)(2,1)} %v_hbm.1, bf16[512,256]{1,0:T(8,128)(2,1)} %do_hbm.1, bf16[3,64,256]{2,1,0:T(8,128)(2,1)} %w_hbm.1, s32[3,512]{1,0:T(4,128)} %bitcast.2, s32[3,512]{1,0:T(4,128)} %bitcast.3, ...), custom_call_target="tpu_custom_call" | custom-call | tf_op jit(solution)/shard_map/pallas_call | solution.py:545
  112.0 1.9 %copy.10 = bf16[512,512]{1,0:T(8,128)(2,1)} copy(bf16[512,512]{1,0:T(8,128)(2,1)} %shard_map.82) | data formatting | bytes 1048576
